TPU v7x, 32 devices: a whole 2x2x4 slice. The times are simulated.
32 devices in a mesh: deme: 8 (over z, y), gen: 4 (over x, core).
Axes of the slice: x: 2, y: 2, z: 4, core: 2. Of those that a mesh axis runs over, the one named last changes fastest.
Arguments:
- freqs: float32 [2048, 128, 512], P('deme', 'gen'), may hold values from 0 to 1
- start_basis: float32 [512, 128], replicated, may hold values from -0.25 to 0.25
Outputs:
- core: float32 [2048, 128, 128], P('deme', 'gen')
- factor: float32 [512, 128], replicated
All inputs are finite; a program needn't handle non-finite values.
Results may differ from a plain program's by a relative error of at most 0.0003.
Values sent between devices are 32-bit elements; how exact they have to be, the bound alone decides.
A program may use at most 64 MiB of HBM per device.

v0:
```python
import jax
import jax.numpy as jnp
from jax import lax
from jax.sharding import PartitionSpec as P

ITERS = 4


def orthonormal(z):
    small = jnp.dot(z.T, z, precision=lax.Precision.HIGHEST, preferred_element_type=jnp.float32)
    lower = jnp.linalg.cholesky(small)
    return jax.scipy.linalg.solve_triangular(lower, z.T, lower=True).T


def times_basis(matrix, basis):
    return jnp.dot(
        matrix, basis, precision=lax.Precision.HIGHEST, preferred_element_type=jnp.float32
    )


def local(freqs, start_basis):
    deme_count, gen_count, loci = freqs.shape
    demes_all = deme_count * lax.axis_size("deme")
    totals = lax.psum(jnp.sum(freqs, axis=0), "deme")
    centered = (freqs - totals / demes_all).reshape(deme_count * gen_count, loci)
    scale = 1.0 / (demes_all * gen_count * lax.axis_size("gen"))
    basis = start_basis
    gram = (
        lax.psum(
            lax.dot_general(
                centered,
                centered,
                (((0,), (0,)), ((), ())),
                precision=lax.Precision.HIGHEST,
                preferred_element_type=jnp.float32,
            ),
            ("deme", "gen"),
        )
        * scale
    )
    for step in range(ITERS):
        basis = orthonormal(times_basis(gram, basis))
    core = jnp.dot(
        centered, basis, precision=lax.Precision.HIGHEST, preferred_element_type=jnp.float32
    )
    return (core.reshape(deme_count, gen_count, basis.shape[1]), basis)


def solution(mesh):
    in_specs = (P("deme", "gen", None), P())
    out_specs = (P("deme", "gen", None), P())
    return jax.shard_map(local, mesh=mesh, in_specs=in_specs, out_specs=out_specs, check_vma=False)
```

profile of v0, /device:TPU:0, one launch (start us, length us, event | category | flops | bytes accessed | tf_op | source)
XLA Modules:
  0.0 380.3 jit_solution(13363751801560558567)
XLA Ops:
  7.2 0.0 copy-start
  7.2 0.0 all-reduce.3.cloned.1.call-start
  7.2 7.5 %reduce_sum.9 = f32[32,512]{1,0:T(8,128)} reduce(f32[256,32,512]{2,1,0:T(8,128)} %param.5, f32[]{:T(128)} %constant.35.clone.1), dimensions={0}, to_apply=%region_0.0 | reduce | flops 4177920 | bytes 16842756 | tf_op jit(solution)/shard_map/reduce_sum | solution.py:24
  14.7 0.0 all-reduce.3.cloned.1.call-update
  14.7 0.0 all-reduce.5.cloned.1.call-start
  14.8 71.2 %all-reduce.3.cloned.1.call-done = f32[32,512]{1,0:T(8,128)} async-done(((f32[32,512]{1,0:T(8,128)}), f32[32,512]{1,0:T(8,128)}) %all-reduce.3.cloned.1.call-update) | async-done | bytes 65552 | tf_op jit(solution)/shard_map/psum | solution.py:24
  86.0 0.8 broadcast_multiply_fusion
  86.9 32.5 %fusion.6 = f32[512,512]{1,0:T(8,128)} fusion(f32[256,32,512]{2,1,0:T(8,128)} %param.5, f32[32,512]{1,0:T(8,128)S(1)} %broadcast_multiply_fusion), kind=kOutput, calls=%fused_computation.6 | convolution fusion | flops 25773998080 | bytes 17891328 | tf_op jit(solution)/shard_map/dot_general | solution.py:30
  119.3 0.0 all-reduce.5.cloned.1.call-update
  119.3 130.0 %all-reduce.5.cloned.1.call-done = f32[512,512]{1,0:T(8,128)} async-done(((f32[512,512]{1,0:T(8,128)}), f32[512,512]{1,0:T(8,128)}) %all-reduce.5.cloned.1.call-update) | async-done | bytes 1048592 | tf_op jit(solution)/shard_map/psum | solution.py:29
  249.3 0.0 copy-done
  249.3 2.2 fusion.15
  251.5 0.6 fusion.52
  252.1 0.1 copy.6
  252.2 11.7 %cholesky.74 = f32[128,128]{1,0:T(8,128)S(1)} custom-call(f32[128,128]{1,0:T(8,128)S(1)} %fusion.41), custom_call_target="Cholesky" | custom-call | tf_op jit(solution)/shard_map/jit(cholesky)/cholesky | solution.py:11
  264.0 0.6 compare_reduce_fusion.3
  264.6 0.7 fusion.30
  265.3 9.8 %custom-call.8 = f32[1,128,128]{1,2,0:T(8,128)S(1)} custom-call(f32[1,128,128]{2,1,0:T(8,128)S(1)} %fusion.30), custom_call_target="InvertDiagBlocksLowerTriangular" | custom-call | tf_op jit(solution)/shard_map/jit(_solve_triangular)/triangular_solve | solution.py:12
  275.1 0.4 fusion.28
  275.5 2.2 fusion.13
  277.7 0.6 fusion.53
  278.3 0.1 copy.7
  278.5 11.9 %cholesky.85 = f32[128,128]{1,0:T(8,128)S(1)} custom-call(f32[128,128]{1,0:T(8,128)S(1)} %fusion.39), custom_call_target="Cholesky" | custom-call | tf_op jit(solution)/shard_map/jit(cholesky)/cholesky | solution.py:11
  290.4 0.6 compare_reduce_fusion.2
  291.0 0.7 fusion.31
  291.7 9.8 %custom-call.9 = f32[1,128,128]{1,2,0:T(8,128)S(1)} custom-call(f32[1,128,128]{2,1,0:T(8,128)S(1)} %fusion.31), custom_call_target="InvertDiagBlocksLowerTriangular" | custom-call | tf_op jit(solution)/shard_map/jit(_solve_triangular)/triangular_solve | solution.py:12
  301.5 0.4 fusion.26
  301.9 2.2 fusion.11
  304.1 0.6 fusion.54
  304.7 0.1 copy.8
  304.9 11.7 %cholesky.96 = f32[128,128]{1,0:T(8,128)S(1)} custom-call(f32[128,128]{1,0:T(8,128)S(1)} %fusion.37), custom_call_target="Cholesky" | custom-call | tf_op jit(solution)/shard_map/jit(cholesky)/cholesky | solution.py:11
  316.6 0.6 compare_reduce_fusion.1
  317.2 0.7 fusion.32
  317.9 9.8 %custom-call.10 = f32[1,128,128]{1,2,0:T(8,128)S(1)} custom-call(f32[1,128,128]{2,1,0:T(8,128)S(1)} %fusion.32), custom_call_target="InvertDiagBlocksLowerTriangular" | custom-call | tf_op jit(solution)/shard_map/jit(_solve_triangular)/triangular_solve | solution.py:12
  327.7 0.4 fusion.24
  328.1 2.6 fusion.9
  330.8 0.6 fusion.55
  331.4 0.1 copy.9
  331.5 11.7 %cholesky.107 = f32[128,128]{1,0:T(8,128)S(1)} custom-call(f32[128,128]{1,0:T(8,128)S(1)} %fusion.35), custom_call_target="Cholesky" | custom-call | tf_op jit(solution)/shard_map/jit(cholesky)/cholesky | solution.py:11
  343.2 0.6 compare_reduce_fusion
  343.9 0.7 fusion.33
  344.5 9.8 %custom-call.11 = f32[1,128,128]{1,2,0:T(8,128)S(1)} custom-call(f32[1,128,128]{2,1,0:T(8,128)S(1)} %fusion.33), custom_call_target="InvertDiagBlocksLowerTriangular" | custom-call | tf_op jit(solution)/shard_map/jit(_solve_triangular)/triangular_solve | solution.py:12
  354.3 0.4 fusion.22
  354.8 17.7 %fusion = f32[256,32,128]{2,1,0:T(8,128)} fusion(f32[256,32,512]{2,1,0:T(8,128)} %param.5, f32[32,512]{1,0:T(8,128)S(1)} %broadcast_multiply_fusion, f32[128,512]{1,0:T(8,128)S(1)} %fusion.22), kind=kOutput, calls=%fused_computation | convolution fusion | flops 6446645248 | bytes 21299200 | tf_op jit(solution)/shard_map/dot_general | solution.py:43
  372.4 0.8 copy.12
  (8 shorter events, 0.2 us)
Async XLA Ops:
  7.2 242.2 %copy-start = (f32[512,128]{1,0:T(8,128)S(1)}, f32[512,128]{1,0:T(8,128)}, u32[]{:S(2)}) copy-start(f32[512,128]{1,0:T(8,128)} %param.6) | copy-start | bytes 786436
  7.2 78.8 %all-reduce.3.cloned.1.call-start = ((), (), s32[]{:S(2)}) async-start(), calls=%async_computation | async-start | bytes 131072 | tf_op jit(solution)/shard_map/psum | solution.py:24
  14.7 234.6 %all-reduce.5.cloned.1.call-start = ((), (), s32[]{:S(2)}) async-start(), calls=%async_computation.1 | async-start | bytes 2097152 | tf_op jit(solution)/shard_map/psum | solution.py:29
Sparse Core Ops, SparseCore 0:
  14.8 71.1 all-reduce.2
  119.5 129.8 all-reduce.4
where the time goes:
time: 387 us; the launch traced here: 380 us
  waiting for transfers between devices  201 us (52%)
  other arithmetic  100 us (26%)
  matrix products  63.4 us (16%)
  between operations  14.4 us (4%)
    psum x1, waiting for transfers between devices, local(): lax.psum(lax.dot_general(centered, centered, (((0,), (0,)), ((), ())), pr...  130 us
    psum x1, waiting for transfers between devices, local(): totals = lax.psum(jnp.sum(freqs, axis=0), 'deme')  71.2 us
    another operation x12, other arithmetic, orthonormal(): lower = jnp.linalg.cholesky(small)  49.7 us
    another operation x8, other arithmetic, orthonormal(): return jax.scipy.linalg.solve_triangular(lower, z.T, lower=True).T  41.9 us
    dot_general x1, matrix products, local(): lax.dot_general(centered, centered, (((0,), (0,)), ((), ())), precision=l...  32.5 us
    dot_general x1, matrix products, local(): jnp.dot(centered, basis, precision=lax.Precision.HIGHEST, preferred_eleme...  17.7 us
    dot_general x4, matrix products, times_basis(): jnp.dot(matrix, basis, precision=lax.Precision.HIGHEST, preferred_element...  9.24 us
  transfers between devices with their start and end apart: 2, of which 2 were waited for; matrix products, arithmetic and copies ran while one was open for 0% of the time, Pallas kernels for 0%

commit v1 on v0

v1 whole, which is shorter than its diff:
```python
import functools

import jax
import jax.numpy as jnp
from jax import lax
from jax.experimental import pallas as pl
from jax.experimental.pallas import tpu as pltpu
from jax.sharding import PartitionSpec as P

ITERS = 4
MESH = pl.DeviceIdType.MESH
HIGHEST = lax.Precision.HIGHEST
F32 = jnp.float32
BF16 = jnp.bfloat16
LANES = 128


def dot(a, b):
    return jnp.dot(a, b, precision=HIGHEST, preferred_element_type=F32)


def tdot(a, b):
    return lax.dot_general(
        a, b, (((0,), (0,)), ((), ())), precision=HIGHEST, preferred_element_type=F32
    )


def tdot16(a, b):
    return lax.dot_general(a, b, (((0,), (0,)), ((), ())), preferred_element_type=F32)


def split(a):
    hi = a.astype(BF16)
    return hi, (a - hi.astype(F32)).astype(BF16)


def pairs(loci):
    tiles = loci // LANES
    return [(i, j) for i in range(tiles) for j in range(i, tiles)]


def gram_kernel(count, x_ref, g_ref, mu_ref, shift, total, same, cross):
    step = pl.program_id(0)
    demes, gens, loci = x_ref.shape
    half = loci // 2

    @pl.when(step == 0)
    def _():
        shift[...] = jnp.sum(x_ref[...], axis=0) * (1.0 / demes)
        total[...] = jnp.zeros_like(total)
        same[...] = jnp.zeros_like(same)
        cross[...] = jnp.zeros_like(cross)

    moved = x_ref[...] - shift[...][None]
    total[...] += jnp.sum(moved, axis=0)
    hi, lo = split(moved.reshape(demes * gens, loci))
    for i in range(2):
        left = hi[:, i * half : (i + 1) * half]
        same[i * half : (i + 1) * half, i * half :] += tdot16(left, hi[:, i * half :])
        cross[i * half : (i + 1) * half, :] += tdot16(left, lo)

    @pl.when(step == pl.num_programs(0) - 1)
    def _():
        rest = total[...] * (1.0 / count)
        mean = shift[...] + rest
        for j in range(loci // LANES):
            mu_ref[j * gens : (j + 1) * gens, :] = mean[:, j * LANES : (j + 1) * LANES]
        for index, (i, j) in enumerate(pairs(loci)):
            rows, cols = slice(i * LANES, (i + 1) * LANES), slice(j * LANES, (j + 1) * LANES)
            block = same[rows, cols] + cross[rows, cols] + cross[cols, rows].T
            block = block - tdot(rest[:, rows], rest[:, cols]) * count
            g_ref[index * LANES : (index + 1) * LANES, :] = block
        used = len(pairs(loci)) * LANES
        if used < g_ref.shape[0]:
            g_ref[used:, :] = jnp.zeros((g_ref.shape[0] - used, LANES), F32)


def local_gram(freqs, packed):
    demes, gens, loci = freqs.shape
    tile = min(32, demes)
    return pl.pallas_call(
        functools.partial(gram_kernel, demes),
        grid=(demes // tile,),
        in_specs=[pl.BlockSpec((tile, gens, loci), lambda i: (i, 0, 0))],
        out_specs=[
            pl.BlockSpec((packed, LANES), lambda i: (0, 0)),
            pl.BlockSpec((gens * loci // LANES, LANES), lambda i: (0, 0)),
        ],
        out_shape=[
            jax.ShapeDtypeStruct((packed, LANES), F32),
            jax.ShapeDtypeStruct((gens * loci // LANES, LANES), F32),
        ],
        scratch_shapes=[
            pltpu.VMEM((gens, loci), F32),
            pltpu.VMEM((gens, loci), F32),
            pltpu.VMEM((loci, loci), F32),
            pltpu.VMEM((loci, loci), F32),
        ],
        compiler_params=pltpu.CompilerParams(vmem_limit_bytes=40 * 2**20),
        name="local_gram",
    )(freqs)


def reduce_kernel(
    count, nd, nx, loci, g_ref, mu_ref, out_ref, mean_ref,
    acc, got_core, got_x, got_deme, full, got_mu, mean,
    send_core, recv_core, send_x, recv_x, send_deme, recv_deme, send_mu, recv_mu,
    send_core2, recv_core2, send_x2, recv_x2, send_deme2, recv_deme2, send_mu2, recv_mu2,
):
    deme = lax.axis_index("deme")
    gen = lax.axis_index("gen")
    x, core = gen // 2, gen % 2

    def at_core():
        return (deme, x * 2 + (1 - core))

    def at_x(k):
        return (deme, ((x + k) % nx) * 2 + core)

    def at_deme(k):
        return ((deme + k) % nd, gen)

    peers = [at_core()] + [at_x(k) for k in range(1, nx)] + [at_deme(k) for k in range(1, nd)]
    barrier = pltpu.get_barrier_semaphore()
    for peer in peers:
        pl.semaphore_signal(barrier, inc=1, device_id=peer, device_id_type=MESH)
    pl.semaphore_wait(barrier, len(peers))

    def copy(src, dst, send, recv, peer):
        return pltpu.make_async_remote_copy(
            src_ref=src, dst_ref=dst, send_sem=send, recv_sem=recv,
            device_id=peer, device_id_type=MESH,
        )

    def run(copies):
        for c in copies:
            c.start()
        for c in copies:
            c.wait()

    def rows(start, size):
        return pl.ds(pl.multiple_of(start, 8), size)

    mrows = mu_ref.shape[0] // nd
    run([
        copy(mu_ref.at[rows((deme + k) % nd * mrows, mrows)], got_mu.at[k - 1],
             send_mu.at[k - 1], recv_mu.at[k - 1], at_deme(k))
        for k in range(1, nd)
    ])
    own = rows(deme * mrows, mrows)
    value = mu_ref[own, :]
    for k in range(1, nd):
        value = value + got_mu[k - 1]
    mean[own, :] = value * (1.0 / nd)
    run([
        copy(mean.at[own], mean.at[own], send_mu2.at[k - 1], recv_mu2.at[k - 1], at_deme(k))
        for k in range(1, nd)
    ])
    mean_ref[...] = mean[...]

    gens = mu_ref.shape[0] // (loci // LANES)
    apart = mean[...] - mu_ref[...]
    for index, (i, j) in enumerate(pairs(loci)):
        at = slice(index * LANES, (index + 1) * LANES)
        acc[at, :] = g_ref[at, :] + count * tdot(
            apart[i * gens : (i + 1) * gens], apart[j * gens : (j + 1) * gens]
        )
    used = len(pairs(loci)) * LANES
    if used < acc.shape[0]:
        acc[used:, :] = g_ref[used:, :]

    size0 = acc.shape[0] // 2
    size1 = size0 // nx
    size2 = size1 // nd
    run([copy(acc.at[rows((1 - core) * size0, size0)], got_core, send_core, recv_core, at_core())])
    at0 = core * size0
    acc[rows(at0, size0), :] += got_core[...]
    run([
        copy(acc.at[rows(at0 + (x + k) % nx * size1, size1)], got_x.at[k - 1],
             send_x.at[k - 1], recv_x.at[k - 1], at_x(k))
        for k in range(1, nx)
    ])
    at1 = at0 + x * size1
    value = acc[rows(at1, size1), :]
    for k in range(1, nx):
        value = value + got_x[k - 1]
    acc[rows(at1, size1), :] = value
    run([
        copy(acc.at[rows(at1 + (deme + k) % nd * size2, size2)], got_deme.at[k - 1],
             send_deme.at[k - 1], recv_deme.at[k - 1], at_deme(k))
        for k in range(1, nd)
    ])
    at2 = at1 + deme * size2
    value = acc[rows(at2, size2), :]
    for k in range(1, nd):
        value = value + got_deme[k - 1]
    full[rows(at2, size2), :] = value

    mine = full.at[rows(at2, size2)]
    run([
        copy(mine, mine, send_deme2.at[k - 1], recv_deme2.at[k - 1], at_deme(k))
        for k in range(1, nd)
    ])
    mine = full.at[rows(at1, size1)]
    run([copy(mine, mine, send_x2.at[k - 1], recv_x2.at[k - 1], at_x(k)) for k in range(1, nx)])
    mine = full.at[rows(at0, size0)]
    run([copy(mine, mine, send_core2, recv_core2, at_core())])
    out_ref[...] = full[...]


def reduce_all(gram, mu, count, nd, nx, loci):
    packed = gram.shape[0]
    size1 = packed // 2 // nx
    dma = pltpu.SemaphoreType.DMA
    sems = [dma, dma] + [dma((max(nx - 1, 1),))] * 2 + [dma((nd - 1,))] * 4
    return pl.pallas_call(
        functools.partial(reduce_kernel, count, nd, nx, loci),
        in_specs=[pl.BlockSpec(memory_space=pltpu.VMEM)] * 2,
        out_specs=[pl.BlockSpec(memory_space=pltpu.VMEM)] * 2,
        out_shape=[jax.ShapeDtypeStruct(gram.shape, F32), jax.ShapeDtypeStruct(mu.shape, F32)],
        scratch_shapes=[
            pltpu.VMEM((packed, LANES), F32),
            pltpu.VMEM((packed // 2, LANES), F32),
            pltpu.VMEM((max(nx - 1, 1), size1, LANES), F32),
            pltpu.VMEM((nd - 1, size1 // nd, LANES), F32),
            pltpu.VMEM((packed, LANES), F32),
            pltpu.VMEM((nd - 1, mu.shape[0] // nd, LANES), F32),
            pltpu.VMEM(mu.shape, F32),
        ] + sems + sems,
        compiler_params=pltpu.CompilerParams(
            collective_id=0, has_side_effects=True, vmem_limit_bytes=40 * 2**20
        ),
        name="reduce_all",
    )(gram, mu)


def inverse_lower(work, out):
    size = out.shape[0]
    lane = lax.broadcasted_iota(jnp.int32, (8, size), 1)

    def spread(row):
        return jnp.broadcast_to(row, (8, size))

    for panel in range(size // 8):
        first = panel * 8
        block = work[first : first + 8, :]
        columns = [
            jnp.broadcast_to(block[:, first + k : first + k + 1], (8, size)) for k in range(8)
        ]
        entry = {(i, k): spread(columns[k][i : i + 1, :]) for k in range(8) for i in range(k, 8)}
        scale = {}
        for k in range(8):
            scale[k] = lax.rsqrt(entry[k, k])
            for i in range(k + 1, 8):
                entry[i, k] = entry[i, k] * scale[k]
            for j in range(k + 1, 8):
                for i in range(j, 8):
                    entry[i, j] = entry[i, j] - entry[i, k] * entry[j, k]
        left, right = [], []
        for k in range(8):
            a, b = spread(block[k : k + 1, :size]), spread(block[k : k + 1, size:])
            for i in range(k):
                a = a - entry[k, i] * left[i]
                b = b - entry[k, i] * right[i]
            left.append(a * scale[k])
            right.append(b * scale[k])
        sub = lax.broadcasted_iota(jnp.int32, (8, size), 0)
        lefts, rights = left[0], right[0]
        for k in range(1, 8):
            lefts = jnp.where(sub == k, left[k], lefts)
            rights = jnp.where(sub == k, right[k], rights)
        out[first : first + 8, :] = rights
        if first + 8 < size:
            later = jnp.where(lane >= first + 8, lefts, 0.0)
            both = jnp.concatenate([lefts, rights], axis=1)
            work[...] = work[...] - tdot(later, both)


def basis_kernel(scale, g_ref, start_ref, out_ref, gram, work, inverse):
    loci, rank = start_ref.shape
    for index, (i, j) in enumerate(pairs(loci)):
        block = g_ref[index * LANES : (index + 1) * LANES, :] * scale
        gram[i * LANES : (i + 1) * LANES, j * LANES : (j + 1) * LANES] = block
        if i != j:
            gram[j * LANES : (j + 1) * LANES, i * LANES : (i + 1) * LANES] = block.T
    out_ref[...] = start_ref[...]
    row = lax.broadcasted_iota(jnp.int32, (rank, rank), 0)
    column = lax.broadcasted_iota(jnp.int32, (rank, rank), 1)

    def step(_, carry):
        z = dot(gram[...], out_ref[...])
        work[:, :rank] = tdot(z, z)
        work[:, rank:] = jnp.where(row == column, 1.0, 0.0)
        inverse_lower(work, inverse)
        out_ref[...] = lax.dot_general(
            z, inverse[...], (((1,), (1,)), ((), ())), precision=HIGHEST,
            preferred_element_type=F32,
        )
        return carry

    lax.fori_loop(0, ITERS, step, 0)


def find_basis(gram, start, scale):
    loci, rank = start.shape
    return pl.pallas_call(
        functools.partial(basis_kernel, scale),
        in_specs=[pl.BlockSpec(memory_space=pltpu.VMEM)] * 2,
        out_specs=pl.BlockSpec(memory_space=pltpu.VMEM),
        out_shape=jax.ShapeDtypeStruct(start.shape, F32),
        scratch_shapes=[
            pltpu.VMEM((loci, loci), F32),
            pltpu.VMEM((rank, 2 * rank), F32),
            pltpu.VMEM((rank, rank), F32),
        ],
        compiler_params=pltpu.CompilerParams(vmem_limit_bytes=40 * 2**20),
        name="find_basis",
    )(gram, start)


def core_kernel(x_ref, mean_ref, factor_ref, out_ref):
    demes, gens, loci = x_ref.shape
    rank = factor_ref.shape[1]
    mean = jnp.concatenate(
        [mean_ref[j * gens : (j + 1) * gens, :] for j in range(loci // LANES)], axis=1
    )
    hi, lo = split((x_ref[...] - mean[None]).reshape(demes * gens, loci))
    fhi, flo = split(factor_ref[...])
    both = jnp.dot(hi, jnp.concatenate([fhi, flo], axis=1), preferred_element_type=F32)
    value = both[:, :rank] + (both[:, rank:] + jnp.dot(lo, fhi, preferred_element_type=F32))
    out_ref[...] = value.reshape(demes, gens, rank)


def find_core(freqs, mean, factor):
    demes, gens, loci = freqs.shape
    rank = factor.shape[1]
    tile = min(32, demes)
    return pl.pallas_call(
        core_kernel,
        grid=(demes // tile,),
        in_specs=[
            pl.BlockSpec((tile, gens, loci), lambda i: (i, 0, 0)),
            pl.BlockSpec(mean.shape, lambda i: (0, 0)),
            pl.BlockSpec(factor.shape, lambda i: (0, 0)),
        ],
        out_specs=pl.BlockSpec((tile, gens, rank), lambda i: (i, 0, 0)),
        out_shape=jax.ShapeDtypeStruct((demes, gens, rank), F32),
        compiler_params=pltpu.CompilerParams(vmem_limit_bytes=40 * 2**20),
        name="find_core",
    )(freqs, mean, factor)


def solution(mesh):
    nd, ng = mesh.shape["deme"], mesh.shape["gen"]
    nx = ng // 2

    def local(freqs, start_basis):
        demes, gens, loci = freqs.shape
        unit = 8 * nd * ng
        packed = -(-len(pairs(loci)) * LANES // unit) * unit
        gram, mu = local_gram(freqs, packed)
        gram, mean = reduce_all(gram, mu, demes, nd, nx, loci)
        scale = 1.0 / (demes * nd * gens * ng)
        factor = find_basis(gram, start_basis, scale)
        return find_core(freqs, mean, factor), factor

    in_specs = (P("deme", "gen", None), P())
    out_specs = (P("deme", "gen", None), P())
    return jax.shard_map(local, mesh=mesh, in_specs=in_specs, out_specs=out_specs, check_vma=False)
```

time: 387 us -> 114 us (0.29); the launches traced: 380 us -> 113 us
  waiting for transfers between devices: 201 us -> 0 us
  Pallas kernels: 0 us -> 112 us
  other arithmetic: 100 us -> 0 us
  matrix products: 63.4 us -> 0 us
  between operations: 14.4 us -> 0.66 us
    psum x2 -> x0, waiting for transfers between devices: 201 us -> none  [the longest x1 130 us: local(): lax.psum(lax.dot_general(centered, centered, (((0,), (0,)), ((), ())), pr...]
    pallas_call x0 -> x4, Pallas kernels: none -> 112 us  [the longest x1 47.1 us: find_basis(): pl.pallas_call(functools.partial(basis_kernel, scale), in_specs=[pl.Block...]
    another operation x20 -> x0, other arithmetic: 91.6 us -> none  [the longest x12 49.7 us: orthonormal(): lower = jnp.linalg.cholesky(small)]
    dot_general x10 -> x0, matrix products: 61.7 us -> none  [the longest x1 32.5 us: local(): lax.dot_general(centered, centered, (((0,), (0,)), ((), ())), precision=l...]
    reduce_sum x1 -> x0, other arithmetic: 7.47 us -> none  [local(): totals = lax.psum(jnp.sum(freqs, axis=0), 'deme')]
  transfers between devices with their start and end apart: 2 -> 0, of which waited for: 2 -> 0; matrix products, arithmetic and copies ran while one was open for 0% -> 0% of each run, Pallas kernels for 0% -> 0%
where the time goes in v1:
time: 114 us; the launch traced here: 113 us
  Pallas kernels  112 us (98%)
    pallas_call x1, Pallas kernels, find_basis(): pl.pallas_call(functools.partial(basis_kernel, scale), in_specs=[pl.Block...  47.1 us
    pallas_call x1, Pallas kernels, reduce_all(): pl.pallas_call(functools.partial(reduce_kernel, count, nd, nx, loci), in_...  38.5 us
    pallas_call x1, Pallas kernels, local_gram(): pl.pallas_call(functools.partial(gram_kernel, demes), grid=(demes // tile...  14.1 us
    pallas_call x1, Pallas kernels, find_core(): pl.pallas_call(core_kernel, grid=(demes // tile,), in_specs=[pl.BlockSpec...  11.9 us

profile of v1, /device:TPU:0, one launch (start us, length us, event | category | flops | bytes accessed | tf_op | source)
XLA Modules:
  0.0 113.2 jit_solution(13069993067728272839)
XLA Ops:
  0.6 0.0 copy-start.1
  0.6 14.1 %local_gram.1 = (f32[1280,128]{1,0:T(8,128)S(1)}, f32[128,128]{1,0:T(8,128)S(1)}) custom-call(f32[256,32,512]{2,1,0:T(8,128)} %x_ref.3), custom_call_target="tpu_custom_call" | custom-call | tf_op jit(solution)/shard_map/local_gram/pallas_call | solution.py:81
  14.8 38.5 %reduce_all.1 = (f32[1280,128]{1,0:T(8,128)S(1)}, f32[128,128]{1,0:T(8,128)S(1)}) custom-call(f32[1280,128]{1,0:T(8,128)S(1)} %get-tuple-element.6.g_ref, f32[128,128]{1,0:T(8,128)S(1)} %get-tuple-element.7.mu_ref), custom_call_target="tpu_custom_call" | custom-call | tf_op jit(solution)/shard_map/reduce_all/pallas_call | solution.py:216
  53.3 0.0 copy-done.1
  53.3 47.1 %find_basis.1.factor_ref = f32[512,128]{1,0:T(8,128)} custom-call(f32[1280,128]{1,0:T(8,128)S(1)} %get-tuple-element.9.g_ref, f32[512,128]{1,0:T(8,128)S(1)} %copy-done.1), custom_call_target="tpu_custom_call" | custom-call | tf_op jit(solution)/shard_map/find_basis/pallas_call | solution.py:306
  100.4 0.0 copy-start
  100.4 0.9 copy-done
  101.3 11.9 %find_core.1 = f32[256,32,128]{2,1,0:T(8,128)} custom-call(f32[256,32,512]{2,1,0:T(8,128)} %x_ref.3, f32[128,128]{1,0:T(8,128)S(1)} %get-tuple-element.8.mean_ref, f32[512,128]{1,0:T(8,128)S(1)} %copy-done), custom_call_target="tpu_custom_call" | custom-call | tf_op jit(solution)/shard_map/find_core/pallas_call | solution.py:338
Async XLA Ops:
  0.6 52.6 %copy-start.1 = (f32[512,128]{1,0:T(8,128)S(1)}, f32[512,128]{1,0:T(8,128)}, u32[]{:S(2)}) copy-start(f32[512,128]{1,0:T(8,128)} %start_ref.1) | copy-start | bytes 786436
  100.4 0.9 copy-start

commit v2 on v1

--- a/solution.py
+++ b/solution.py
@@ -39,7 +39,7 @@
     return [(i, j) for i in range(tiles) for j in range(i, tiles)]
 
 
-def gram_kernel(count, x_ref, g_ref, mu_ref, shift, total, same, cross):
+def gram_kernel(count, x_ref, g_ref, mu_ref, shift, total, upper, lower):
     step = pl.program_id(0)
     demes, gens, loci = x_ref.shape
     half = loci // 2
@@ -48,16 +48,28 @@
     def _():
         shift[...] = jnp.sum(x_ref[...], axis=0) * (1.0 / demes)
         total[...] = jnp.zeros_like(total)
-        same[...] = jnp.zeros_like(same)
-        cross[...] = jnp.zeros_like(cross)
+        upper[...] = jnp.zeros_like(upper)
+        lower[...] = jnp.zeros_like(lower)
 
     moved = x_ref[...] - shift[...][None]
     total[...] += jnp.sum(moved, axis=0)
     hi, lo = split(moved.reshape(demes * gens, loci))
-    for i in range(2):
-        left = hi[:, i * half : (i + 1) * half]
-        same[i * half : (i + 1) * half, i * half :] += tdot16(left, hi[:, i * half :])
-        cross[i * half : (i + 1) * half, :] += tdot16(left, lo)
+    upper[...] += tdot16(hi[:, :half], jnp.concatenate([hi, lo], axis=1))
+    lower[...] += tdot16(hi[:, half:], jnp.concatenate([hi[:, half:], lo], axis=1))
+
+    def same(i, j):
+        if i < half // LANES:
+            return upper[i * LANES : (i + 1) * LANES, j * LANES : (j + 1) * LANES]
+        return lower[
+            i * LANES - half : (i + 1) * LANES - half, j * LANES - half : (j + 1) * LANES - half
+        ]
+
+    def cross(i, j):
+        if i < half // LANES:
+            return upper[i * LANES : (i + 1) * LANES, loci + j * LANES : loci + (j + 1) * LANES]
+        return lower[
+            i * LANES - half : (i + 1) * LANES - half, half + j * LANES : half + (j + 1) * LANES
+        ]
 
     @pl.when(step == pl.num_programs(0) - 1)
     def _():
@@ -67,7 +79,7 @@
             mu_ref[j * gens : (j + 1) * gens, :] = mean[:, j * LANES : (j + 1) * LANES]
         for index, (i, j) in enumerate(pairs(loci)):
             rows, cols = slice(i * LANES, (i + 1) * LANES), slice(j * LANES, (j + 1) * LANES)
-            block = same[rows, cols] + cross[rows, cols] + cross[cols, rows].T
+            block = same(i, j) + (cross(i, j) + cross(j, i).T)
             block = block - tdot(rest[:, rows], rest[:, cols]) * count
             g_ref[index * LANES : (index + 1) * LANES, :] = block
         used = len(pairs(loci)) * LANES
@@ -93,8 +105,8 @@
         scratch_shapes=[
             pltpu.VMEM((gens, loci), F32),
             pltpu.VMEM((gens, loci), F32),
-            pltpu.VMEM((loci, loci), F32),
-            pltpu.VMEM((loci, loci), F32),
+            pltpu.VMEM((loci // 2, 2 * loci), F32),
+            pltpu.VMEM((loci // 2, loci + loci // 2), F32),
         ],
         compiler_params=pltpu.CompilerParams(vmem_limit_bytes=40 * 2**20),
         name="local_gram",
@@ -234,68 +246,103 @@
     )(gram, mu)
 
 
-def inverse_lower(work, out):
-    size = out.shape[0]
-    lane = lax.broadcasted_iota(jnp.int32, (8, size), 1)
+def inverse_lower(matrix):
+    size = matrix.shape[0]
+    shape = (8, size)
+    lane = lax.broadcasted_iota(jnp.int32, shape, 1)
+    sub = lax.broadcasted_iota(jnp.int32, shape, 0)
 
     def spread(row):
-        return jnp.broadcast_to(row, (8, size))
-
-    for panel in range(size // 8):
+        return jnp.broadcast_to(row, shape)
+
+    tiles = [matrix[t * 8 : t * 8 + 8, :] for t in range(size // 8)]
+    done = []
+    for panel in range(len(tiles)):
         first = panel * 8
-        block = work[first : first + 8, :]
+        inside = (lane >= first) & (lane < first + 8)
         columns = [
-            jnp.broadcast_to(block[:, first + k : first + k + 1], (8, size)) for k in range(8)
+            [jnp.broadcast_to(tile[:, first + k : first + k + 1], shape) for k in range(8)]
+            for tile in tiles[panel:]
         ]
-        entry = {(i, k): spread(columns[k][i : i + 1, :]) for k in range(8) for i in range(k, 8)}
-        scale = {}
+        entry = {(i, k): spread(columns[0][k][i : i + 1, :]) for k in range(8) for i in range(k, 8)}
+        base = jnp.where(inside, jnp.where(lane == first + sub, 1.0, 0.0), tiles[panel])
+        scale, rows = [], []
         for k in range(8):
-            scale[k] = lax.rsqrt(entry[k, k])
+            scale.append(lax.rsqrt(entry[k, k]))
             for i in range(k + 1, 8):
                 entry[i, k] = entry[i, k] * scale[k]
             for j in range(k + 1, 8):
                 for i in range(j, 8):
                     entry[i, j] = entry[i, j] - entry[i, k] * entry[j, k]
-        left, right = [], []
         for k in range(8):
-            a, b = spread(block[k : k + 1, :size]), spread(block[k : k + 1, size:])
+            row = spread(base[k : k + 1, :])
             for i in range(k):
-                a = a - entry[k, i] * left[i]
-                b = b - entry[k, i] * right[i]
-            left.append(a * scale[k])
-            right.append(b * scale[k])
-        sub = lax.broadcasted_iota(jnp.int32, (8, size), 0)
-        lefts, rights = left[0], right[0]
+                row = row - entry[k, i] * rows[i]
+            rows.append(row * scale[k])
+        block = rows[0]
         for k in range(1, 8):
-            lefts = jnp.where(sub == k, left[k], lefts)
-            rights = jnp.where(sub == k, right[k], rights)
-        out[first : first + 8, :] = rights
-        if first + 8 < size:
-            later = jnp.where(lane >= first + 8, lefts, 0.0)
-            both = jnp.concatenate([lefts, rights], axis=1)
-            work[...] = work[...] - tdot(later, both)
-
-
-def basis_kernel(scale, g_ref, start_ref, out_ref, gram, work, inverse):
+            block = jnp.where(sub == k, rows[k], block)
+        done.append(jnp.where(lane < first + 8, block, 0.0))
+        for t in range(panel + 1, len(tiles)):
+            column = columns[t - panel]
+            tile = jnp.where(inside, 0.0, tiles[t])
+            lower = []
+            for k in range(8):
+                value = column[k]
+                for i in range(k):
+                    value = value - lower[i] * entry[k, i]
+                lower.append(value * scale[k])
+                tile = tile - lower[k] * rows[k]
+            tiles[t] = tile
+    return jnp.concatenate(done, axis=0)
+
+
+def split3(a):
+    one = a.astype(BF16)
+    rest = a - one.astype(F32)
+    two = rest.astype(BF16)
+    return one, two, (rest - two.astype(F32)).astype(BF16)
+
+
+def dot16(a, b):
+    return jnp.dot(a, b, preferred_element_type=F32)
+
+
+def basis_kernel(scale, g_ref, start_ref, out_ref, gram1, gram2, gram3):
     loci, rank = start_ref.shape
     for index, (i, j) in enumerate(pairs(loci)):
         block = g_ref[index * LANES : (index + 1) * LANES, :] * scale
-        gram[i * LANES : (i + 1) * LANES, j * LANES : (j + 1) * LANES] = block
+        rows, cols = slice(i * LANES, (i + 1) * LANES), slice(j * LANES, (j + 1) * LANES)
+        for ref, piece in zip((gram1, gram2, gram3), split3(block)):
+            ref[rows, cols] = piece
         if i != j:
-            gram[j * LANES : (j + 1) * LANES, i * LANES : (i + 1) * LANES] = block.T
+            for ref, piece in zip((gram1, gram2, gram3), split3(block.T)):
+                ref[cols, rows] = piece
     out_ref[...] = start_ref[...]
-    row = lax.broadcasted_iota(jnp.int32, (rank, rank), 0)
-    column = lax.broadcasted_iota(jnp.int32, (rank, rank), 1)
 
     def step(_, carry):
-        z = dot(gram[...], out_ref[...])
-        work[:, :rank] = tdot(z, z)
-        work[:, rank:] = jnp.where(row == column, 1.0, 0.0)
-        inverse_lower(work, inverse)
-        out_ref[...] = lax.dot_general(
-            z, inverse[...], (((1,), (1,)), ((), ())), precision=HIGHEST,
+        q1, q2, q3 = split3(out_ref[...])
+        both = jnp.concatenate([q1, q2], axis=1)
+        large, small = dot16(gram1[...], both), dot16(gram2[...], both)
+        rest = dot16(gram1[...], q3) + dot16(gram3[...], q1)
+        z = large[:, :rank] + (large[:, rank:] + (small[:, :rank] + (small[:, rank:] + rest)))
+        z1, z2, z3 = split3(z)
+        both = jnp.concatenate([z1, z2], axis=1)
+        square = tdot16(both, both)
+        rest = tdot16(z1, z3)
+        rest = rest + rest.T + square[rank:, rank:]
+        small = square[:rank, :rank] + (square[:rank, rank:] + (square[rank:, :rank] + rest))
+        w1, w2, w3 = split3(inverse_lower(small))
+        right = jnp.concatenate(
+            [jnp.concatenate([w1, w1], axis=1), jnp.concatenate([w2, w2], axis=1)], axis=0
+        )
+        contract = (((1,), (1,)), ((), ()))
+        large = lax.dot_general(both, right, contract, preferred_element_type=F32)
+        rest = lax.dot_general(
+            jnp.concatenate([z3, z1], axis=1), jnp.concatenate([w1, w3], axis=1), contract,
             preferred_element_type=F32,
         )
+        out_ref[...] = large[:, :rank] + (large[:, rank:] + rest)
         return carry
 
     lax.fori_loop(0, ITERS, step, 0)
@@ -309,9 +356,9 @@
         out_specs=pl.BlockSpec(memory_space=pltpu.VMEM),
         out_shape=jax.ShapeDtypeStruct(start.shape, F32),
         scratch_shapes=[
-            pltpu.VMEM((loci, loci), F32),
-            pltpu.VMEM((rank, 2 * rank), F32),
-            pltpu.VMEM((rank, rank), F32),
+            pltpu.VMEM((loci, loci), BF16),
+            pltpu.VMEM((loci, loci), BF16),
+            pltpu.VMEM((loci, loci), BF16),
         ],
         compiler_params=pltpu.CompilerParams(vmem_limit_bytes=40 * 2**20),
         name="find_basis",
@@ -324,11 +371,14 @@
     mean = jnp.concatenate(
         [mean_ref[j * gens : (j + 1) * gens, :] for j in range(loci // LANES)], axis=1
     )
-    hi, lo = split((x_ref[...] - mean[None]).reshape(demes * gens, loci))
     fhi, flo = split(factor_ref[...])
-    both = jnp.dot(hi, jnp.concatenate([fhi, flo], axis=1), preferred_element_type=F32)
-    value = both[:, :rank] + (both[:, rank:] + jnp.dot(lo, fhi, preferred_element_type=F32))
-    out_ref[...] = value.reshape(demes, gens, rank)
+    pieces = jnp.concatenate([fhi, flo], axis=1)
+    part = 8 if demes % 8 == 0 else demes
+    for at in range(0, demes, part):
+        hi, lo = split((x_ref[at : at + part] - mean[None]).reshape(part * gens, loci))
+        both = dot16(hi, pieces)
+        value = both[:, :rank] + (both[:, rank:] + dot16(lo, fhi))
+        out_ref[at : at + part] = value.reshape(part, gens, rank)
 
 
 def find_core(freqs, mean, factor):

time: 114 us -> 92 us (0.81)
  Pallas kernels: 112 us -> 90 us
    pallas_call x1, Pallas kernels: 47.1 us -> 25.5 us  [find_basis(): pl.pallas_call(functools.partial(basis_kernel, scale), in_specs=[pl.Block...]
where the time goes in v2:
time: 92 us; the launch traced here: 91.6 us
  Pallas kernels  90 us (98%)
  local copies, waits for them, and re-layouts  0.95 us (1%)
    pallas_call x1, Pallas kernels, reduce_all(): pl.pallas_call(functools.partial(reduce_kernel, count, nd, nx, loci), in_...  38.5 us
    pallas_call x1, Pallas kernels, find_basis(): pl.pallas_call(functools.partial(basis_kernel, scale), in_specs=[pl.Block...  25.5 us
    pallas_call x1, Pallas kernels, local_gram(): pl.pallas_call(functools.partial(gram_kernel, demes), grid=(demes // tile...  14.1 us
    pallas_call x1, Pallas kernels, find_core(): pl.pallas_call(core_kernel, grid=(demes // tile,), in_specs=[pl.BlockSpec...  11.9 us

profile of v2, /device:TPU:0, one launch (start us, length us, event | category | flops | bytes accessed | tf_op | source)
XLA Modules:
  0.0 91.6 jit_solution(2853977097873037296)
XLA Ops:
  0.6 0.0 copy-start.1
  0.6 14.1 %local_gram.1 = (f32[1280,128]{1,0:T(8,128)S(1)}, f32[128,128]{1,0:T(8,128)S(1)}) custom-call(f32[256,32,512]{2,1,0:T(8,128)} %x_ref.3), custom_call_target="tpu_custom_call" | custom-call | tf_op jit(solution)/shard_map/local_gram/pallas_call | solution.py:93
  14.8 38.5 %reduce_all.1 = (f32[1280,128]{1,0:T(8,128)S(1)}, f32[128,128]{1,0:T(8,128)S(1)}) custom-call(f32[1280,128]{1,0:T(8,128)S(1)} %get-tuple-element.6.g_ref, f32[128,128]{1,0:T(8,128)S(1)} %get-tuple-element.7.mu_ref), custom_call_target="tpu_custom_call" | custom-call | tf_op jit(solution)/shard_map/reduce_all/pallas_call | solution.py:228
  53.3 0.0 copy-done.1
  53.3 25.5 %find_basis.1.factor_ref = f32[512,128]{1,0:T(8,128)} custom-call(f32[1280,128]{1,0:T(8,128)S(1)} %get-tuple-element.9.g_ref, f32[512,128]{1,0:T(8,128)S(1)} %copy-done.1), custom_call_target="tpu_custom_call" | custom-call | tf_op jit(solution)/shard_map/find_basis/pallas_call | solution.py:353
  78.8 0.0 copy-start
  78.8 0.9 %copy-done = f32[512,128]{1,0:T(8,128)S(1)} copy-done((f32[512,128]{1,0:T(8,128)S(1)}, f32[512,128]{1,0:T(8,128)}, u32[]{:S(2)}) %copy-start) | copy-done | bytes 262168
  79.7 11.9 %find_core.1 = f32[256,32,128]{2,1,0:T(8,128)} custom-call(f32[256,32,512]{2,1,0:T(8,128)} %x_ref.3, f32[128,128]{1,0:T(8,128)S(1)} %get-tuple-element.8.mean_ref, f32[512,128]{1,0:T(8,128)S(1)} %copy-done), custom_call_target="tpu_custom_call" | custom-call | tf_op jit(solution)/shard_map/find_core/pallas_call | solution.py:388
Async XLA Ops:
  0.6 52.6 %copy-start.1 = (f32[512,128]{1,0:T(8,128)S(1)}, f32[512,128]{1,0:T(8,128)}, u32[]{:S(2)}) copy-start(f32[512,128]{1,0:T(8,128)} %start_ref.1) | copy-start | bytes 786436
  78.8 0.9 %copy-start = (f32[512,128]{1,0:T(8,128)S(1)}, f32[512,128]{1,0:T(8,128)}, u32[]{:S(2)}) copy-start(f32[512,128]{1,0:T(8,128)} %find_basis.1.factor_ref) | copy-start | bytes 786436

commit v3 on v2

v3 whole, which is shorter than its diff:
```python
import functools

import jax
import jax.numpy as jnp
from jax import lax
from jax.experimental import pallas as pl
from jax.experimental.pallas import tpu as pltpu
from jax.sharding import PartitionSpec as P

ITERS = 4
MESH = pl.DeviceIdType.MESH
HIGHEST = lax.Precision.HIGHEST
F32 = jnp.float32
BF16 = jnp.bfloat16
LANES = 128


def dot(a, b):
    return jnp.dot(a, b, precision=HIGHEST, preferred_element_type=F32)


def tdot(a, b):
    return lax.dot_general(
        a, b, (((0,), (0,)), ((), ())), precision=HIGHEST, preferred_element_type=F32
    )


def tdot16(a, b):
    return lax.dot_general(a, b, (((0,), (0,)), ((), ())), preferred_element_type=F32)


def split(a):
    hi = a.astype(BF16)
    return hi, (a - hi.astype(F32)).astype(BF16)


def pairs(loci):
    tiles = loci // LANES
    return [(i, j) for i in range(tiles) for j in range(i, tiles)]


def chains(unit):
    first = unit // 16 * 8
    return [first, unit - first] if first else [unit]


def gram_kernel(
    nd, nx, x_ref, out_ref, mean_ref, kept,
    shift, total, upper, lower, mu, mean, got_mu, acc, got_core, got_x, got_deme, full,
    load, send_mu, recv_mu, send_mu2, recv_mu2,
    send_core, recv_core, send_x, recv_x, send_deme, recv_deme,
    send_core2, recv_core2, send_x2, recv_x2, send_deme2, recv_deme2,
):
    demes, gens, loci = x_ref.shape
    half = loci // 2
    parts = load.shape[0]
    tile = demes // parts
    deme = lax.axis_index("deme")
    gen = lax.axis_index("gen")
    x, core = gen // 2, gen % 2

    def at_core():
        return (deme, x * 2 + (1 - core))

    def at_x(k):
        return (deme, ((x + k) % nx) * 2 + core)

    def at_deme(k):
        return ((deme + k) % nd, gen)

    peers = [at_core()] + [at_x(k) for k in range(1, nx)] + [at_deme(k) for k in range(1, nd)]
    barrier = pltpu.get_barrier_semaphore()
    for peer in peers:
        pl.semaphore_signal(barrier, inc=1, device_id=peer, device_id_type=MESH)

    def copy(src, dst, send, recv, peer):
        return pltpu.make_async_remote_copy(
            src_ref=src, dst_ref=dst, send_sem=send, recv_sem=recv,
            device_id=peer, device_id_type=MESH,
        )

    def start(copies):
        for c in copies:
            c.start()
        return copies

    def wait(copies):
        for c in copies:
            c.wait()

    def rows(first, size):
        return pl.ds(pl.multiple_of(first, 8), size)

    loads = start([
        pltpu.make_async_copy(
            x_ref.at[pl.ds(i * tile, tile)], kept.at[pl.ds(i * tile, tile)], load.at[i]
        )
        for i in range(parts)
    ])

    def add_sum(i):
        loads[i].wait()
        total[...] += jnp.sum(kept[i * tile : (i + 1) * tile], axis=0)

    def add_gram(i):
        moved = kept[pl.ds(i * tile, tile)] - shift[...][None]
        hi, lo = split(moved.reshape(tile * gens, loci))
        upper[...] += tdot16(hi[:, :half], jnp.concatenate([hi, lo], axis=1))
        lower[...] += tdot16(hi[:, half:], jnp.concatenate([hi[:, half:], lo], axis=1))

    def grams(first, last):
        def body(i, carry):
            add_gram(i)
            return carry

        lax.fori_loop(first, last, body, 0)

    total[...] = jnp.zeros_like(total)
    upper[...] = jnp.zeros_like(upper)
    lower[...] = jnp.zeros_like(lower)
    add_sum(0)
    shift[...] = total[...] * (1.0 / tile)
    early = parts // 4
    for i in range(1, parts // 2):
        add_sum(i)
    grams(0, early)
    for i in range(max(parts // 2, 1), parts):
        add_sum(i)
    tiles = loci // LANES
    own_mean = total[...] * (1.0 / demes)
    for j in range(tiles):
        mu[j * gens : (j + 1) * gens, :] = own_mean[:, j * LANES : (j + 1) * LANES]
    rest = own_mean - shift[...]

    pl.semaphore_wait(barrier, len(peers))
    mrows = mu.shape[0] // nd
    sent = start([
        copy(mu.at[rows((deme + k) % nd * mrows, mrows)], got_mu.at[k - 1],
             send_mu.at[k - 1], recv_mu.at[k - 1], at_deme(k))
        for k in range(1, nd)
    ])
    middle = (early + parts + 1) // 2
    grams(early, middle)
    wait(sent)
    own = rows(deme * mrows, mrows)
    value = mu[own, :]
    for k in range(1, nd):
        value = value + got_mu[k - 1]
    mean[own, :] = value * (1.0 / nd)
    sent = start([
        copy(mean.at[own], mean.at[own], send_mu2.at[k - 1], recv_mu2.at[k - 1], at_deme(k))
        for k in range(1, nd)
    ])
    grams(middle, parts)
    wait(sent)
    mean_ref[...] = mean[...]

    def same(i, j):
        if i < half // LANES:
            return upper[i * LANES : (i + 1) * LANES, j * LANES : (j + 1) * LANES]
        return lower[
            i * LANES - half : (i + 1) * LANES - half, j * LANES - half : (j + 1) * LANES - half
        ]

    def cross(i, j):
        if i < half // LANES:
            return upper[i * LANES : (i + 1) * LANES, loci + j * LANES : loci + (j + 1) * LANES]
        return lower[
            i * LANES - half : (i + 1) * LANES - half, half + j * LANES : half + (j + 1) * LANES
        ]

    apart = [
        mean[j * gens : (j + 1) * gens, :] - mu[j * gens : (j + 1) * gens, :] for j in range(tiles)
    ]
    moved = [rest[:, j * LANES : (j + 1) * LANES] for j in range(tiles)]
    left = [jnp.concatenate([a, b], axis=0) for a, b in zip(apart, moved)]
    right = [jnp.concatenate([a, -b], axis=0) for a, b in zip(apart, moved)]
    for index, (i, j) in enumerate(pairs(loci)):
        block = same(i, j) + (cross(i, j) + cross(j, i).T)
        acc[index * LANES : (index + 1) * LANES, :] = block + demes * tdot(left[i], right[j])
    used = len(pairs(loci)) * LANES
    if used < acc.shape[0]:
        acc[used:, :] = jnp.zeros((acc.shape[0] - used, LANES), F32)

    def steps(c, base, unit):
        size1 = unit * nd
        size0 = size1 * nx
        at0 = base * nd * nx * 2 + core * size0
        other0 = base * nd * nx * 2 + (1 - core) * size0
        at1 = at0 + x * size1
        at2 = at1 + deme * unit
        part0 = got_core.at[pl.ds(base * nd * nx, size0)]
        part1 = [got_x.at[k - 1, pl.ds(base * nd, size1)] for k in range(1, nx)]
        part2 = [got_deme.at[k - 1, pl.ds(base, unit)] for k in range(1, nd)]
        sent = start([
            copy(acc.at[rows(other0, size0)], part0, send_core.at[c], recv_core.at[c], at_core())
        ])
        yield
        wait(sent)
        acc[rows(at0, size0), :] += part0[...]
        sent = start([
            copy(acc.at[rows(at0 + (x + k) % nx * size1, size1)], part1[k - 1],
                 send_x.at[c, k - 1], recv_x.at[c, k - 1], at_x(k))
            for k in range(1, nx)
        ])
        yield
        wait(sent)
        value = acc[rows(at1, size1), :]
        for part in part1:
            value = value + part[...]
        acc[rows(at1, size1), :] = value
        sent = start([
            copy(acc.at[rows(at1 + (deme + k) % nd * unit, unit)], part2[k - 1],
                 send_deme.at[c, k - 1], recv_deme.at[c, k - 1], at_deme(k))
            for k in range(1, nd)
        ])
        yield
        wait(sent)
        value = acc[rows(at2, unit), :]
        for part in part2:
            value = value + part[...]
        full[rows(at2, unit), :] = value
        mine = full.at[rows(at2, unit)]
        sent = start([
            copy(mine, mine, send_deme2.at[c, k - 1], recv_deme2.at[c, k - 1], at_deme(k))
            for k in range(1, nd)
        ])
        yield
        wait(sent)
        mine1 = full.at[rows(at1, size1)]
        sent = start([
            copy(mine1, mine1, send_x2.at[c, k - 1], recv_x2.at[c, k - 1], at_x(k))
            for k in range(1, nx)
        ])
        yield
        wait(sent)
        mine0 = full.at[rows(at0, size0)]
        sent = start([copy(mine0, mine0, send_core2.at[c], recv_core2.at[c], at_core())])
        yield
        wait(sent)
        yield

    running, base = [], 0
    for c, unit in enumerate(chains(got_deme.shape[1])):
        running.append(steps(c, base, unit))
        base += unit
    for _ in range(7):
        for chain in running:
            next(chain)
    out_ref[...] = full[...]


def sum_gram(freqs, packed, nd, nx):
    demes, gens, loci = freqs.shape
    parts = 8 if demes % 8 == 0 else 1
    unit = packed // (2 * nx * nd)
    count = len(chains(unit))
    mshape = (gens * loci // LANES, LANES)
    far = max(nx - 1, 1)
    dma = pltpu.SemaphoreType.DMA
    sems = [dma((count,))] * 2 + [dma((count, far))] * 2 + [dma((count, nd - 1))] * 2
    vmem = pl.BlockSpec(memory_space=pltpu.VMEM)
    return pl.pallas_call(
        functools.partial(gram_kernel, nd, nx),
        in_specs=[pl.BlockSpec(memory_space=pl.ANY)],
        out_specs=[vmem, vmem, vmem],
        out_shape=[
            jax.ShapeDtypeStruct((packed, LANES), F32),
            jax.ShapeDtypeStruct(mshape, F32),
            pltpu.VMEM(freqs.shape, F32),
        ],
        scratch_shapes=[
            pltpu.VMEM((gens, loci), F32),
            pltpu.VMEM((gens, loci), F32),
            pltpu.VMEM((loci // 2, 2 * loci), F32),
            pltpu.VMEM((loci // 2, loci + loci // 2), F32),
            pltpu.VMEM(mshape, F32),
            pltpu.VMEM(mshape, F32),
            pltpu.VMEM((nd - 1, mshape[0] // nd, LANES), F32),
            pltpu.VMEM((packed, LANES), F32),
            pltpu.VMEM((packed // 2, LANES), F32),
            pltpu.VMEM((far, unit * nd, LANES), F32),
            pltpu.VMEM((nd - 1, unit, LANES), F32),
            pltpu.VMEM((packed, LANES), F32),
            dma((parts,)),
        ] + [dma((nd - 1,))] * 4 + sems + sems,
        compiler_params=pltpu.CompilerParams(
            collective_id=0, has_side_effects=True, vmem_limit_bytes=30 * 2**20
        ),
        name="sum_gram",
    )(freqs)


def inverse_lower(matrix):
    size = matrix.shape[0]
    shape = (8, size)
    lane = lax.broadcasted_iota(jnp.int32, shape, 1)
    sub = lax.broadcasted_iota(jnp.int32, shape, 0)

    def spread(row):
        return jnp.broadcast_to(row, shape)

    tiles = [matrix[t * 8 : t * 8 + 8, :] for t in range(size // 8)]
    done = []
    for panel in range(len(tiles)):
        first = panel * 8
        inside = (lane >= first) & (lane < first + 8)
        columns = [
            [jnp.broadcast_to(tile[:, first + k : first + k + 1], shape) for k in range(8)]
            for tile in tiles[panel:]
        ]
        entry = {(i, k): spread(columns[0][k][i : i + 1, :]) for k in range(8) for i in range(k, 8)}
        base = jnp.where(inside, jnp.where(lane == first + sub, 1.0, 0.0), tiles[panel])
        scale, rows = [], []
        for k in range(8):
            scale.append(lax.rsqrt(entry[k, k]))
            for i in range(k + 1, 8):
                entry[i, k] = entry[i, k] * scale[k]
            for j in range(k + 1, 8):
                for i in range(j, 8):
                    entry[i, j] = entry[i, j] - entry[i, k] * entry[j, k]
        for k in range(8):
            row = spread(base[k : k + 1, :])
            for i in range(k):
                row = row - entry[k, i] * rows[i]
            rows.append(row * scale[k])
        block = rows[0]
        for k in range(1, 8):
            block = jnp.where(sub == k, rows[k], block)
        done.append(jnp.where(lane < first + 8, block, 0.0))
        for t in range(panel + 1, len(tiles)):
            column = columns[t - panel]
            tile = jnp.where(inside, 0.0, tiles[t])
            lower = []
            for k in range(8):
                value = column[k]
                for i in range(k):
                    value = value - lower[i] * entry[k, i]
                lower.append(value * scale[k])
                tile = tile - lower[k] * rows[k]
            tiles[t] = tile
    return jnp.concatenate(done, axis=0)


def split3(a):
    one = a.astype(BF16)
    rest = a - one.astype(F32)
    two = rest.astype(BF16)
    return one, two, (rest - two.astype(F32)).astype(BF16)


def dot16(a, b):
    return jnp.dot(a, b, preferred_element_type=F32)


def basis_kernel(scale, g_ref, start_ref, out_ref, kept, gram1, gram2, gram3):
    loci, rank = start_ref.shape
    for index, (i, j) in enumerate(pairs(loci)):
        block = g_ref[index * LANES : (index + 1) * LANES, :] * scale
        rows, cols = slice(i * LANES, (i + 1) * LANES), slice(j * LANES, (j + 1) * LANES)
        for ref, piece in zip((gram1, gram2, gram3), split3(block)):
            ref[rows, cols] = piece
        if i != j:
            for ref, piece in zip((gram1, gram2, gram3), split3(block.T)):
                ref[cols, rows] = piece
    out_ref[...] = start_ref[...]

    def step(_, carry):
        q1, q2, q3 = split3(out_ref[...])
        both = jnp.concatenate([q1, q2], axis=1)
        large, small = dot16(gram1[...], both), dot16(gram2[...], both)
        rest = dot16(gram1[...], q3) + dot16(gram3[...], q1)
        z = large[:, :rank] + (large[:, rank:] + (small[:, :rank] + (small[:, rank:] + rest)))
        z1, z2, z3 = split3(z)
        both = jnp.concatenate([z1, z2], axis=1)
        square = tdot16(both, both)
        rest = tdot16(z1, z3)
        rest = rest + rest.T + square[rank:, rank:]
        small = square[:rank, :rank] + (square[:rank, rank:] + (square[rank:, :rank] + rest))
        w1, w2, w3 = split3(inverse_lower(small))
        right = jnp.concatenate(
            [jnp.concatenate([w1, w1], axis=1), jnp.concatenate([w2, w2], axis=1)], axis=0
        )
        contract = (((1,), (1,)), ((), ()))
        large = lax.dot_general(both, right, contract, preferred_element_type=F32)
        rest = lax.dot_general(
            jnp.concatenate([z3, z1], axis=1), jnp.concatenate([w1, w3], axis=1), contract,
            preferred_element_type=F32,
        )
        out_ref[...] = large[:, :rank] + (large[:, rank:] + rest)
        return carry

    lax.fori_loop(0, ITERS, step, 0)
    kept[...] = out_ref[...]


def find_basis(gram, start, scale):
    loci, rank = start.shape
    return pl.pallas_call(
        functools.partial(basis_kernel, scale),
        in_specs=[pl.BlockSpec(memory_space=pltpu.VMEM)] * 2,
        out_specs=[pl.BlockSpec(memory_space=pltpu.VMEM)] * 2,
        out_shape=[jax.ShapeDtypeStruct(start.shape, F32), pltpu.VMEM(start.shape, F32)],
        scratch_shapes=[
            pltpu.VMEM((loci, loci), BF16),
            pltpu.VMEM((loci, loci), BF16),
            pltpu.VMEM((loci, loci), BF16),
        ],
        compiler_params=pltpu.CompilerParams(vmem_limit_bytes=30 * 2**20),
        name="find_basis",
    )(gram, start)


def core_kernel(x_ref, mean_ref, factor_ref, out_ref):
    demes, gens, rank = out_ref.shape
    loci = x_ref.shape[2]
    mean = jnp.concatenate(
        [mean_ref[j * gens : (j + 1) * gens, :] for j in range(loci // LANES)], axis=1
    )
    fhi, flo = split(factor_ref[...])
    pieces = jnp.concatenate([fhi, flo], axis=1)
    part = 8 if demes % 8 == 0 else demes
    first = pl.program_id(0) * demes
    for at in range(0, demes, part):
        hi, lo = split((x_ref[pl.ds(first + at, part)] - mean[None]).reshape(part * gens, loci))
        both = dot16(hi, pieces)
        value = both[:, :rank] + (both[:, rank:] + dot16(lo, fhi))
        out_ref[at : at + part] = value.reshape(part, gens, rank)


def find_core(freqs, mean, factor):
    demes, gens, loci = freqs.shape
    rank = factor.shape[1]
    tile = 32 if demes % 32 == 0 else demes
    vmem = pl.BlockSpec(memory_space=pltpu.VMEM)
    return pl.pallas_call(
        core_kernel,
        grid=(demes // tile,),
        in_specs=[vmem, vmem, vmem],
        out_specs=pl.BlockSpec((tile, gens, rank), lambda i: (i, 0, 0)),
        out_shape=jax.ShapeDtypeStruct((demes, gens, rank), F32),
        compiler_params=pltpu.CompilerParams(vmem_limit_bytes=30 * 2**20),
        name="find_core",
    )(pltpu.with_memory_space_constraint(freqs, pltpu.VMEM), mean, factor)


def solution(mesh):
    nd, ng = mesh.shape["deme"], mesh.shape["gen"]
    nx = ng // 2

    def local(freqs, start_basis):
        demes, gens, loci = freqs.shape
        unit = 8 * nd * ng
        packed = -(-len(pairs(loci)) * LANES // unit) * unit
        gram, mean, kept = sum_gram(freqs, packed, nd, nx)
        scale = 1.0 / (demes * nd * gens * ng)
        factor, near = find_basis(gram, start_basis, scale)
        return find_core(kept, mean, near), factor

    in_specs = (P("deme", "gen", None), P())
    out_specs = (P("deme", "gen", None), P())
    return jax.shard_map(local, mesh=mesh, in_specs=in_specs, out_specs=out_specs, check_vma=False)
```

time: 92 us -> 73.7 us (0.80)
  Pallas kernels: 90 us -> 72.9 us
  local copies, waits for them, and re-layouts: 0.95 us -> 0.01 us
    pallas_call x3 -> x2, Pallas kernels: 64.5 us -> 47.4 us  [the longest x1 40.6 us: sum_gram(): pl.pallas_call(functools.partial(gram_kernel, nd, nx), in_specs=[pl.Block...]
    unnamed x4 -> x2, local copies, waits for them, and re-layouts: 0.95 us -> 0.01 us
where the time goes in v3:
time: 73.7 us; the launch traced here: 73.5 us
  Pallas kernels  72.9 us (99%)
    pallas_call x1, Pallas kernels, sum_gram(): pl.pallas_call(functools.partial(gram_kernel, nd, nx), in_specs=[pl.Block...  40.6 us
    pallas_call x1, Pallas kernels, find_basis(): pl.pallas_call(functools.partial(basis_kernel, scale), in_specs=[pl.Block...  25.5 us
    pallas_call x1, Pallas kernels, find_core(): pl.pallas_call(core_kernel, grid=(demes // tile,), in_specs=[vmem, vmem,...  6.71 us

profile of v3, /device:TPU:0, one launch (start us, length us, event | category | flops | bytes accessed | tf_op | source)
XLA Modules:
  0.0 73.5 jit_solution(11313462251361902742)
XLA Ops:
  0.6 0.0 copy-start
  0.6 40.6 %sum_gram.1 = (f32[1280,128]{1,0:T(8,128)S(1)}, f32[128,128]{1,0:T(8,128)S(1)}, f32[256,32,512]{2,1,0:T(8,128)S(1)}) custom-call(f32[256,32,512]{2,1,0:T(8,128)} %x_ref.1), custom_call_target="tpu_custom_call" | custom-call | tf_op jit(solution)/shard_map/sum_gram/pallas_call | solution.py:263
  41.3 0.0 copy-done
  41.3 25.5 %find_basis.1 = (f32[512,128]{1,0:T(8,128)}, f32[512,128]{1,0:T(8,128)S(1)}) custom-call(f32[1280,128]{1,0:T(8,128)S(1)} %get-tuple-element.9.g_ref, f32[512,128]{1,0:T(8,128)S(1)} %copy-done), custom_call_target="tpu_custom_call" | custom-call | tf_op jit(solution)/shard_map/find_basis/pallas_call | solution.py:399
  66.8 6.7 %find_core.1 = f32[256,32,128]{2,1,0:T(8,128)} custom-call(f32[256,32,512]{2,1,0:T(8,128)S(1)} %get-tuple-element.7.x_ref, f32[128,128]{1,0:T(8,128)S(1)} %get-tuple-element.8.mean_ref, f32[512,128]{1,0:T(8,128)S(1)} %get-tuple-element.10.factor_ref), custom_call_target="tpu_custom_call" | custom-call | tf_op jit(solution)/shard_map/find_core/pallas_call | solution.py:436
Async XLA Ops:
  0.6 40.7 %copy-start = (f32[512,128]{1,0:T(8,128)S(1)}, f32[512,128]{1,0:T(8,128)}, u32[]{:S(2)}) copy-start(f32[512,128]{1,0:T(8,128)} %start_ref.1) | copy-start | bytes 786436

commit v4 on v3

--- a/solution.py
+++ b/solution.py
@@ -45,9 +45,10 @@
 
 
 def gram_kernel(
-    nd, nx, x_ref, out_ref, mean_ref, kept,
-    shift, total, upper, lower, mu, mean, got_mu, acc, got_core, got_x, got_deme, full,
-    load, send_mu, recv_mu, send_mu2, recv_mu2,
+    nd, nx, x_ref, out_ref, offset_ref, hi_ref, lo_ref,
+    loaded, shift, total, upper, swapped, lower, mu, mean, got_mu, mu2, mean2, apart,
+    acc, got_core, got_x, got_deme, full,
+    load, send_mu, recv_mu, send_mean, recv_mean, send_mean2, recv_mean2, send_other, recv_other,
     send_core, recv_core, send_x, recv_x, send_deme, recv_deme,
     send_core2, recv_core2, send_x2, recv_x2, send_deme2, recv_deme2,
 ):
@@ -68,7 +69,11 @@
     def at_deme(k):
         return ((deme + k) % nd, gen)
 
-    peers = [at_core()] + [at_x(k) for k in range(1, nx)] + [at_deme(k) for k in range(1, nd)]
+    def at_other(k):
+        return ((deme + k) % nd, x * 2 + (1 - core))
+
+    peers = [at_core()] + [at_x(k) for k in range(1, nx)]
+    peers += [at(k) for k in range(1, nd) for at in (at_deme, at_other)]
     barrier = pltpu.get_barrier_semaphore()
     for peer in peers:
         pl.semaphore_signal(barrier, inc=1, device_id=peer, device_id_type=MESH)
@@ -93,39 +98,48 @@
 
     loads = start([
         pltpu.make_async_copy(
-            x_ref.at[pl.ds(i * tile, tile)], kept.at[pl.ds(i * tile, tile)], load.at[i]
+            x_ref.at[pl.ds(i * tile, tile)], loaded.at[pl.ds(i * tile, tile)], load.at[i]
         )
         for i in range(parts)
     ])
+    size = tile * gens
 
     def add_sum(i):
         loads[i].wait()
-        total[...] += jnp.sum(kept[i * tile : (i + 1) * tile], axis=0)
-
-    def add_gram(i):
-        moved = kept[pl.ds(i * tile, tile)] - shift[...][None]
-        hi, lo = split(moved.reshape(tile * gens, loci))
+        total[...] += jnp.sum(loaded[i * tile : (i + 1) * tile], axis=0)
+
+    def cut(i):
+        moved = loaded[i * tile : (i + 1) * tile] - shift[...][None]
+        hi, lo = split(moved.reshape(size, loci))
+        hi_ref[i * size : (i + 1) * size, :] = hi
+        lo_ref[i * size : (i + 1) * size, :] = lo
+
+    def add_upper(i):
+        hi, lo = hi_ref[i * size : (i + 1) * size, :], lo_ref[i * size : (i + 1) * size, :]
         upper[...] += tdot16(hi[:, :half], jnp.concatenate([hi, lo], axis=1))
-        lower[...] += tdot16(hi[:, half:], jnp.concatenate([hi[:, half:], lo], axis=1))
-
-    def grams(first, last):
+        swapped[...] += tdot16(lo[:, :half], hi[:, half:])
+
+    def add_lower(first, last):
         def body(i, carry):
-            add_gram(i)
+            at = pl.ds(pl.multiple_of(i * size, size), size)
+            hi, lo = hi_ref[at, half:], lo_ref[at, half:]
+            lower[...] += tdot16(hi, jnp.concatenate([hi, lo], axis=1))
             return carry
 
         lax.fori_loop(first, last, body, 0)
 
     total[...] = jnp.zeros_like(total)
     upper[...] = jnp.zeros_like(upper)
+    swapped[...] = jnp.zeros_like(swapped)
     lower[...] = jnp.zeros_like(lower)
     add_sum(0)
     shift[...] = total[...] * (1.0 / tile)
-    early = parts // 4
-    for i in range(1, parts // 2):
+    cut(0)
+    for i in range(1, parts):
         add_sum(i)
-    grams(0, early)
-    for i in range(max(parts // 2, 1), parts):
-        add_sum(i)
+        cut(i)
+        if i < parts - 1:
+            add_upper(i - 1)
     tiles = loci // LANES
     own_mean = total[...] * (1.0 / demes)
     for j in range(tiles):
@@ -139,48 +153,65 @@
              send_mu.at[k - 1], recv_mu.at[k - 1], at_deme(k))
         for k in range(1, nd)
     ])
-    middle = (early + parts + 1) // 2
-    grams(early, middle)
+    sent_other = start([copy(mu, mu2, send_other, recv_other, at_core())])
+    for i in range(max(parts - 2, 0), parts):
+        add_upper(i)
     wait(sent)
     own = rows(deme * mrows, mrows)
     value = mu[own, :]
     for k in range(1, nd):
         value = value + got_mu[k - 1]
     mean[own, :] = value * (1.0 / nd)
-    sent = start([
-        copy(mean.at[own], mean.at[own], send_mu2.at[k - 1], recv_mu2.at[k - 1], at_deme(k))
+    sent_mean = start([
+        copy(mean.at[own], mean.at[own], send_mean.at[k - 1], recv_mean.at[k - 1], at_deme(k))
         for k in range(1, nd)
+    ] + [
+        copy(mean.at[own], mean2.at[own], send_mean2.at[k], recv_mean2.at[k], at_other(k))
+        for k in range(nd)
     ])
-    grams(middle, parts)
-    wait(sent)
-    mean_ref[...] = mean[...]
-
-    def same(i, j):
-        if i < half // LANES:
-            return upper[i * LANES : (i + 1) * LANES, j * LANES : (j + 1) * LANES]
-        return lower[
-            i * LANES - half : (i + 1) * LANES - half, j * LANES - half : (j + 1) * LANES - half
-        ]
-
-    def cross(i, j):
-        if i < half // LANES:
-            return upper[i * LANES : (i + 1) * LANES, loci + j * LANES : loci + (j + 1) * LANES]
-        return lower[
-            i * LANES - half : (i + 1) * LANES - half, half + j * LANES : half + (j + 1) * LANES
-        ]
-
-    apart = [
-        mean[j * gens : (j + 1) * gens, :] - mu[j * gens : (j + 1) * gens, :] for j in range(tiles)
-    ]
-    moved = [rest[:, j * LANES : (j + 1) * LANES] for j in range(tiles)]
-    left = [jnp.concatenate([a, b], axis=0) for a, b in zip(apart, moved)]
-    right = [jnp.concatenate([a, -b], axis=0) for a, b in zip(apart, moved)]
-    for index, (i, j) in enumerate(pairs(loci)):
-        block = same(i, j) + (cross(i, j) + cross(j, i).T)
-        acc[index * LANES : (index + 1) * LANES, :] = block + demes * tdot(left[i], right[j])
-    used = len(pairs(loci)) * LANES
+
+    def block(i, j):
+        rows_, cols = slice(i * LANES, (i + 1) * LANES), slice(j * LANES, (j + 1) * LANES)
+        across = slice(j * LANES - half, (j + 1) * LANES - half)
+        if i >= half // LANES:
+            first = slice(i * LANES - half, (i + 1) * LANES - half)
+            again = slice(j * LANES, (j + 1) * LANES)
+            value = lower[first, across] + (
+                lower[first, again] + lower[across, i * LANES : (i + 1) * LANES].T
+            )
+        elif j >= half // LANES:
+            value = upper[rows_, cols] + (
+                upper[rows_, loci + j * LANES : loci + (j + 1) * LANES] + swapped[rows_, across]
+            )
+        else:
+            value = upper[rows_, cols] + (
+                upper[rows_, loci + j * LANES : loci + (j + 1) * LANES]
+                + upper[cols, loci + i * LANES : loci + (i + 1) * LANES].T
+            )
+        return value - demes * tdot(rest[:, rows_], rest[:, cols])
+
+    blocks = pairs(loci)
+
+    def put(indices):
+        for index in indices:
+            acc[index * LANES : (index + 1) * LANES, :] = block(*blocks[index])
+
+    early = [index for index, (i, j) in enumerate(blocks) if i < half // LANES]
+    late = [index for index, (i, j) in enumerate(blocks) if i >= half // LANES]
+    put(early)
+    used = len(blocks) * LANES
     if used < acc.shape[0]:
         acc[used:, :] = jnp.zeros((acc.shape[0] - used, LANES), F32)
+
+    def correct(at0, first, count):
+        for index in range(count):
+            here = [blocks[b] if b < len(blocks) else (0, 0)
+                    for b in (first + index, first + count + index)]
+            i = jnp.where(core == 0, here[0][0], here[1][0])
+            j = jnp.where(core == 0, here[0][1], here[1][1])
+            left = apart[rows(i * 2 * gens, 2 * gens), :]
+            right = apart[rows(j * 2 * gens, 2 * gens), :]
+            acc[rows(at0 + index * LANES, LANES), :] += demes * tdot(left, right)
 
     def steps(c, base, unit):
         size1 = unit * nd
@@ -198,6 +229,8 @@
         yield
         wait(sent)
         acc[rows(at0, size0), :] += part0[...]
+        yield
+        correct(at0, base * nd * nx * 2 // LANES, size0 // LANES)
         sent = start([
             copy(acc.at[rows(at0 + (x + k) % nx * size1, size1)], part1[k - 1],
                  send_x.at[c, k - 1], recv_x.at[c, k - 1], at_x(k))
@@ -240,11 +273,31 @@
         wait(sent)
         yield
 
-    running, base = [], 0
+    running, base, ends = [], 0, []
     for c, unit in enumerate(chains(got_deme.shape[1])):
         running.append(steps(c, base, unit))
         base += unit
-    for _ in range(7):
+        ends.append(base * nd * nx * 2 // LANES)
+    ahead = [chain for chain, end in zip(running, ends) if end <= len(early)]
+    for chain in ahead:
+        next(chain)
+    add_lower(0, parts)
+    put(late)
+    for chain in running:
+        if chain not in ahead:
+            next(chain)
+    for chain in running:
+        next(chain)
+    wait(sent_other)
+    wait(sent_mean)
+    for j in range(tiles):
+        at = slice(j * gens, (j + 1) * gens)
+        offset_ref[:, j * LANES : (j + 1) * LANES] = (
+            mean[at, :] - shift[:, j * LANES : (j + 1) * LANES]
+        )
+        apart[j * 2 * gens : j * 2 * gens + gens, :] = mean[at, :] - mu[at, :]
+        apart[j * 2 * gens + gens : (j + 1) * 2 * gens, :] = mean2[at, :] - mu2[at, :]
+    for _ in range(6):
         for chain in running:
             next(chain)
     out_ref[...] = full[...]
@@ -263,29 +316,35 @@
     return pl.pallas_call(
         functools.partial(gram_kernel, nd, nx),
         in_specs=[pl.BlockSpec(memory_space=pl.ANY)],
-        out_specs=[vmem, vmem, vmem],
+        out_specs=[vmem] * 4,
         out_shape=[
             jax.ShapeDtypeStruct((packed, LANES), F32),
-            jax.ShapeDtypeStruct(mshape, F32),
-            pltpu.VMEM(freqs.shape, F32),
+            jax.ShapeDtypeStruct((gens, loci), F32),
+            pltpu.VMEM((demes * gens, loci), BF16),
+            pltpu.VMEM((demes * gens, loci), BF16),
         ],
         scratch_shapes=[
+            pltpu.VMEM(freqs.shape, F32),
             pltpu.VMEM((gens, loci), F32),
             pltpu.VMEM((gens, loci), F32),
             pltpu.VMEM((loci // 2, 2 * loci), F32),
-            pltpu.VMEM((loci // 2, loci + loci // 2), F32),
+            pltpu.VMEM((loci // 2, loci // 2), F32),
+            pltpu.VMEM((loci // 2, loci), F32),
             pltpu.VMEM(mshape, F32),
             pltpu.VMEM(mshape, F32),
             pltpu.VMEM((nd - 1, mshape[0] // nd, LANES), F32),
+            pltpu.VMEM(mshape, F32),
+            pltpu.VMEM(mshape, F32),
+            pltpu.VMEM((2 * mshape[0], LANES), F32),
             pltpu.VMEM((packed, LANES), F32),
             pltpu.VMEM((packed // 2, LANES), F32),
             pltpu.VMEM((far, unit * nd, LANES), F32),
             pltpu.VMEM((nd - 1, unit, LANES), F32),
             pltpu.VMEM((packed, LANES), F32),
             dma((parts,)),
-        ] + [dma((nd - 1,))] * 4 + sems + sems,
+        ] + [dma((nd - 1,))] * 4 + [dma((nd,))] * 2 + [dma] * 2 + sems + sems,
         compiler_params=pltpu.CompilerParams(
-            collective_id=0, has_side_effects=True, vmem_limit_bytes=30 * 2**20
+            collective_id=0, has_side_effects=True, vmem_limit_bytes=32 * 2**20
         ),
         name="sum_gram",
     )(freqs)
@@ -312,13 +371,20 @@
         entry = {(i, k): spread(columns[0][k][i : i + 1, :]) for k in range(8) for i in range(k, 8)}
         base = jnp.where(inside, jnp.where(lane == first + sub, 1.0, 0.0), tiles[panel])
         scale, rows = [], []
-        for k in range(8):
-            scale.append(lax.rsqrt(entry[k, k]))
+        for k in range(0, 8, 2):
+            pivot, beside = entry[k, k], entry[k + 1, k]
+            det = pivot * entry[k + 1, k + 1] - beside * beside
+            first_scale = lax.rsqrt(pivot)
+            scale += [first_scale, (pivot * first_scale) * lax.rsqrt(det)]
             for i in range(k + 1, 8):
-                entry[i, k] = entry[i, k] * scale[k]
-            for j in range(k + 1, 8):
+                entry[i, k] = entry[i, k] * first_scale
+            for i in range(k + 2, 8):
+                entry[i, k + 1] = (entry[i, k + 1] - entry[i, k] * entry[k + 1, k]) * scale[k + 1]
+            for j in range(k + 2, 8):
                 for i in range(j, 8):
-                    entry[i, j] = entry[i, j] - entry[i, k] * entry[j, k]
+                    entry[i, j] = (entry[i, j] - entry[i, k] * entry[j, k]) - (
+                        entry[i, k + 1] * entry[j, k + 1]
+                    )
         for k in range(8):
             row = spread(base[k : k + 1, :])
             for i in range(k):
@@ -353,8 +419,18 @@
     return jnp.dot(a, b, preferred_element_type=F32)
 
 
-def basis_kernel(scale, g_ref, start_ref, out_ref, kept, gram1, gram2, gram3):
+def basis_kernel(g_ref, start_ref, out_ref, kept, gram1, gram2, gram3):
     loci, rank = start_ref.shape
+    on = lax.broadcasted_iota(jnp.int32, (LANES, LANES), 0) == lax.broadcasted_iota(
+        jnp.int32, (LANES, LANES), 1
+    )
+    largest = jnp.zeros((LANES, LANES), F32)
+    for index, (i, j) in enumerate(pairs(loci)):
+        if i == j:
+            block = g_ref[index * LANES : (index + 1) * LANES, :]
+            largest = jnp.maximum(largest, jnp.where(on, block, 0.0))
+    largest = jnp.max(jnp.max(largest, axis=0, keepdims=True), axis=1, keepdims=True)
+    scale = 1.0 / largest
     for index, (i, j) in enumerate(pairs(loci)):
         block = g_ref[index * LANES : (index + 1) * LANES, :] * scale
         rows, cols = slice(i * LANES, (i + 1) * LANES), slice(j * LANES, (j + 1) * LANES)
@@ -394,10 +470,10 @@
     kept[...] = out_ref[...]
 
 
-def find_basis(gram, start, scale):
+def find_basis(gram, start):
     loci, rank = start.shape
     return pl.pallas_call(
-        functools.partial(basis_kernel, scale),
+        basis_kernel,
         in_specs=[pl.BlockSpec(memory_space=pltpu.VMEM)] * 2,
         out_specs=[pl.BlockSpec(memory_space=pltpu.VMEM)] * 2,
         out_shape=[jax.ShapeDtypeStruct(start.shape, F32), pltpu.VMEM(start.shape, F32)],
@@ -406,42 +482,43 @@
             pltpu.VMEM((loci, loci), BF16),
             pltpu.VMEM((loci, loci), BF16),
         ],
-        compiler_params=pltpu.CompilerParams(vmem_limit_bytes=30 * 2**20),
+        compiler_params=pltpu.CompilerParams(vmem_limit_bytes=16 * 2**20),
         name="find_basis",
     )(gram, start)
 
 
-def core_kernel(x_ref, mean_ref, factor_ref, out_ref):
+def core_kernel(hi_ref, lo_ref, offset_ref, factor_ref, out_ref):
     demes, gens, rank = out_ref.shape
-    loci = x_ref.shape[2]
-    mean = jnp.concatenate(
-        [mean_ref[j * gens : (j + 1) * gens, :] for j in range(loci // LANES)], axis=1
-    )
     fhi, flo = split(factor_ref[...])
     pieces = jnp.concatenate([fhi, flo], axis=1)
+    ohi, olo = split(offset_ref[...])
+    both = dot16(ohi, pieces)
+    offset = both[:, :rank] + (both[:, rank:] + dot16(olo, fhi))
     part = 8 if demes % 8 == 0 else demes
-    first = pl.program_id(0) * demes
+    size = part * gens
+    first = pl.program_id(0) * demes * gens
     for at in range(0, demes, part):
-        hi, lo = split((x_ref[pl.ds(first + at, part)] - mean[None]).reshape(part * gens, loci))
-        both = dot16(hi, pieces)
-        value = both[:, :rank] + (both[:, rank:] + dot16(lo, fhi))
-        out_ref[at : at + part] = value.reshape(part, gens, rank)
-
-
-def find_core(freqs, mean, factor):
-    demes, gens, loci = freqs.shape
-    rank = factor.shape[1]
+        here = pl.ds(pl.multiple_of(first + at * gens, size), size)
+        both = dot16(hi_ref[here, :], pieces)
+        value = both[:, :rank] + (both[:, rank:] + dot16(lo_ref[here, :], fhi))
+        out_ref[at : at + part] = value.reshape(part, gens, rank) - offset[None]
+
+
+def find_core(hi, lo, offset, factor):
+    gens, rank = offset.shape[0], factor.shape[1]
+    demes = hi.shape[0] // gens
     tile = 32 if demes % 32 == 0 else demes
     vmem = pl.BlockSpec(memory_space=pltpu.VMEM)
+    hi, lo = (pltpu.with_memory_space_constraint(a, pltpu.VMEM) for a in (hi, lo))
     return pl.pallas_call(
         core_kernel,
         grid=(demes // tile,),
-        in_specs=[vmem, vmem, vmem],
+        in_specs=[vmem] * 4,
         out_specs=pl.BlockSpec((tile, gens, rank), lambda i: (i, 0, 0)),
         out_shape=jax.ShapeDtypeStruct((demes, gens, rank), F32),
-        compiler_params=pltpu.CompilerParams(vmem_limit_bytes=30 * 2**20),
+        compiler_params=pltpu.CompilerParams(vmem_limit_bytes=16 * 2**20),
         name="find_core",
-    )(pltpu.with_memory_space_constraint(freqs, pltpu.VMEM), mean, factor)
+    )(hi, lo, offset, factor)
 
 
 def solution(mesh):
@@ -452,10 +529,9 @@
         demes, gens, loci = freqs.shape
         unit = 8 * nd * ng
         packed = -(-len(pairs(loci)) * LANES // unit) * unit
-        gram, mean, kept = sum_gram(freqs, packed, nd, nx)
-        scale = 1.0 / (demes * nd * gens * ng)
-        factor, near = find_basis(gram, start_basis, scale)
-        return find_core(kept, mean, near), factor
+        gram, offset, hi, lo = sum_gram(freqs, packed, nd, nx)
+        factor, near = find_basis(gram, start_basis)
+        return find_core(hi, lo, offset, near), factor
 
     in_specs = (P("deme", "gen", None), P())
     out_specs = (P("deme", "gen", None), P())

time: 73.7 us -> 81.7 us (1.11)
  Pallas kernels: 72.9 us -> 80.9 us
    pallas_call x1, Pallas kernels: 40.6 us -> 48.4 us  [sum_gram(): pl.pallas_call(functools.partial(gram_kernel, nd, nx), in_specs=[pl.Block...]
where the time goes in v4:
time: 81.7 us; the launch traced here: 81.6 us
  Pallas kernels  80.9 us (99%)
    pallas_call x1, Pallas kernels, sum_gram(): pl.pallas_call(functools.partial(gram_kernel, nd, nx), in_specs=[pl.Block...  48.4 us
    pallas_call x1, Pallas kernels, find_basis(): pl.pallas_call(basis_kernel, in_specs=[pl.BlockSpec(memory_space=pltpu.VM...  25.5 us
    pallas_call x1, Pallas kernels, find_core(): pl.pallas_call(core_kernel, grid=(demes // tile,), in_specs=[vmem] * 4, o...  7.02 us

profile of v4, /device:TPU:0, one launch (start us, length us, event | category | flops | bytes accessed | tf_op | source)
XLA Modules:
  0.0 81.6 jit_solution(8973621324144755547)
XLA Ops:
  0.6 0.0 copy-start
  0.6 48.4 %sum_gram.1 = (f32[1280,128]{1,0:T(8,128)S(1)}, f32[32,512]{1,0:T(8,128)S(1)}, bf16[8192,512]{1,0:T(8,128)(2,1)S(1)}, bf16[8192,512]{1,0:T(8,128)(2,1)S(1)}) custom-call(f32[256,32,512]{2,1,0:T(8,128)} %x_ref.1), custom_call_target="tpu_custom_call" | custom-call | tf_op jit(solution)/shard_map/sum_gram/pallas_call | solution.py:316
  49.1 0.0 copy-done
  49.1 25.5 %find_basis.1 = (f32[512,128]{1,0:T(8,128)}, f32[512,128]{1,0:T(8,128)S(1)}) custom-call(f32[1280,128]{1,0:T(8,128)S(1)} %get-tuple-element.11.g_ref, f32[512,128]{1,0:T(8,128)S(1)} %copy-done), custom_call_target="tpu_custom_call" | custom-call | tf_op jit(solution)/shard_map/find_basis/pallas_call | solution.py:475
  74.5 7.0 %find_core.1 = f32[256,32,128]{2,1,0:T(8,128)} custom-call(bf16[8192,512]{1,0:T(8,128)(2,1)S(1)} %get-tuple-element.8.hi_ref, bf16[8192,512]{1,0:T(8,128)(2,1)S(1)} %get-tuple-element.9.lo_ref, f32[32,512]{1,0:T(8,128)S(1)} %get-tuple-element.10.offset_ref, f32[512,128]{1,0:T(8,128)S(1)} %get-tuple-element.12.factor_ref), custom_call_target="tpu_custom_call" | custom-call | tf_op jit(solution)/shard_map/find_core/pallas_call | solution.py:513
Async XLA Ops:
  0.6 48.4 %copy-start = (f32[512,128]{1,0:T(8,128)S(1)}, f32[512,128]{1,0:T(8,128)}, u32[]{:S(2)}) copy-start(f32[512,128]{1,0:T(8,128)} %start_ref.1) | copy-start | bytes 786436

commit v5 on v3

--- a/solution.py
+++ b/solution.py
@@ -105,8 +105,8 @@
     def add_gram(i):
         moved = kept[pl.ds(i * tile, tile)] - shift[...][None]
         hi, lo = split(moved.reshape(tile * gens, loci))
-        upper[...] += tdot16(hi[:, :half], jnp.concatenate([hi, lo], axis=1))
-        lower[...] += tdot16(hi[:, half:], jnp.concatenate([hi[:, half:], lo], axis=1))
+        upper[...] += tdot16(jnp.concatenate([hi, lo], axis=1), hi[:, :half])
+        lower[...] += tdot16(jnp.concatenate([hi[:, half:], lo], axis=1), hi[:, half:])
 
     def grams(first, last):
         def body(i, carry):
@@ -155,19 +155,10 @@
     wait(sent)
     mean_ref[...] = mean[...]
 
-    def same(i, j):
-        if i < half // LANES:
-            return upper[i * LANES : (i + 1) * LANES, j * LANES : (j + 1) * LANES]
-        return lower[
-            i * LANES - half : (i + 1) * LANES - half, j * LANES - half : (j + 1) * LANES - half
-        ]
-
-    def cross(i, j):
-        if i < half // LANES:
-            return upper[i * LANES : (i + 1) * LANES, loci + j * LANES : loci + (j + 1) * LANES]
-        return lower[
-            i * LANES - half : (i + 1) * LANES - half, half + j * LANES : half + (j + 1) * LANES
-        ]
+    def piece(first, j):
+        if j < half // LANES:
+            return upper[first : first + LANES, j * LANES : (j + 1) * LANES]
+        return lower[first - half : first - half + LANES, j * LANES - half : (j + 1) * LANES - half]
 
     apart = [
         mean[j * gens : (j + 1) * gens, :] - mu[j * gens : (j + 1) * gens, :] for j in range(tiles)
@@ -176,7 +167,8 @@
     left = [jnp.concatenate([a, b], axis=0) for a, b in zip(apart, moved)]
     right = [jnp.concatenate([a, -b], axis=0) for a, b in zip(apart, moved)]
     for index, (i, j) in enumerate(pairs(loci)):
-        block = same(i, j) + (cross(i, j) + cross(j, i).T)
+        block = piece(j * LANES, i) + piece(loci + j * LANES, i)
+        block = block.T + piece(loci + i * LANES, j)
         acc[index * LANES : (index + 1) * LANES, :] = block + demes * tdot(left[i], right[j])
     used = len(pairs(loci)) * LANES
     if used < acc.shape[0]:
@@ -272,8 +264,8 @@
         scratch_shapes=[
             pltpu.VMEM((gens, loci), F32),
             pltpu.VMEM((gens, loci), F32),
-            pltpu.VMEM((loci // 2, 2 * loci), F32),
-            pltpu.VMEM((loci // 2, loci + loci // 2), F32),
+            pltpu.VMEM((2 * loci, loci // 2), F32),
+            pltpu.VMEM((loci + loci // 2, loci // 2), F32),
             pltpu.VMEM(mshape, F32),
             pltpu.VMEM(mshape, F32),
             pltpu.VMEM((nd - 1, mshape[0] // nd, LANES), F32),
@@ -301,13 +293,14 @@
         return jnp.broadcast_to(row, shape)
 
     tiles = [matrix[t * 8 : t * 8 + 8, :] for t in range(size // 8)]
-    done = []
+    done, blocks, group = [], [], 4
     for panel in range(len(tiles)):
         first = panel * 8
+        end = min((panel // group + 1) * group, len(tiles))
         inside = (lane >= first) & (lane < first + 8)
         columns = [
             [jnp.broadcast_to(tile[:, first + k : first + k + 1], shape) for k in range(8)]
-            for tile in tiles[panel:]
+            for tile in tiles[panel:end]
         ]
         entry = {(i, k): spread(columns[0][k][i : i + 1, :]) for k in range(8) for i in range(k, 8)}
         base = jnp.where(inside, jnp.where(lane == first + sub, 1.0, 0.0), tiles[panel])
@@ -328,7 +321,7 @@
         for k in range(1, 8):
             block = jnp.where(sub == k, rows[k], block)
         done.append(jnp.where(lane < first + 8, block, 0.0))
-        for t in range(panel + 1, len(tiles)):
+        for t in range(panel + 1, end):
             column = columns[t - panel]
             tile = jnp.where(inside, 0.0, tiles[t])
             lower = []
@@ -339,6 +332,15 @@
                 lower.append(value * scale[k])
                 tile = tile - lower[k] * rows[k]
             tiles[t] = tile
+        blocks.append(block)
+        if panel + 1 == end and end < len(tiles):
+            later = lane >= end * 8
+            left = [jnp.where(later, b, 0.0) for b in blocks[-group:]]
+            right = [jnp.where(later, b, d) for b, d in zip(blocks[-group:], done[-group:])]
+            change = tdot(jnp.concatenate(left, axis=0), jnp.concatenate(right, axis=0))
+            inside = (lane >= (end - group) * 8) & (lane < end * 8)
+            for t in range(end, len(tiles)):
+                tiles[t] = jnp.where(inside, 0.0, tiles[t]) - change[t * 8 : t * 8 + 8, :]
     return jnp.concatenate(done, axis=0)
 
 
@@ -419,7 +421,7 @@
     )
     fhi, flo = split(factor_ref[...])
     pieces = jnp.concatenate([fhi, flo], axis=1)
-    part = 8 if demes % 8 == 0 else demes
+    part = demes
     first = pl.program_id(0) * demes
     for at in range(0, demes, part):
         hi, lo = split((x_ref[pl.ds(first + at, part)] - mean[None]).reshape(part * gens, loci))

time: 73.7 us -> 71.7 us (0.973)
  Pallas kernels: 72.9 us -> 70.9 us
    pallas_call x1, Pallas kernels: 25.5 us -> 24.2 us  [find_basis(): pl.pallas_call(functools.partial(basis_kernel, scale), in_specs=[pl.Block...]
    pallas_call x1, Pallas kernels: 40.6 us -> 39.8 us  [sum_gram(): pl.pallas_call(functools.partial(gram_kernel, nd, nx), in_specs=[pl.Block...]
where the time goes in v5:
time: 71.7 us; the launch traced here: 71.5 us
  Pallas kernels  70.9 us (99%)
    pallas_call x1, Pallas kernels, sum_gram(): pl.pallas_call(functools.partial(gram_kernel, nd, nx), in_specs=[pl.Block...  39.8 us
    pallas_call x1, Pallas kernels, find_basis(): pl.pallas_call(functools.partial(basis_kernel, scale), in_specs=[pl.Block...  24.2 us
    pallas_call x1, Pallas kernels, find_core(): pl.pallas_call(core_kernel, grid=(demes // tile,), in_specs=[vmem, vmem,...  6.77 us

profile of v5, /device:TPU:0, one launch (start us, length us, event | category | flops | bytes accessed | tf_op | source)
XLA Modules:
  0.0 71.5 jit_solution(17141225561341949227)
XLA Ops:
  0.6 0.0 copy-start
  0.6 39.8 %sum_gram.1 = (f32[1280,128]{1,0:T(8,128)S(1)}, f32[128,128]{1,0:T(8,128)S(1)}, f32[256,32,512]{2,1,0:T(8,128)S(1)}) custom-call(f32[256,32,512]{2,1,0:T(8,128)} %x_ref.1), custom_call_target="tpu_custom_call" | custom-call | tf_op jit(solution)/shard_map/sum_gram/pallas_call | solution.py:255
  40.5 0.0 copy-done
  40.5 24.2 %find_basis.1 = (f32[512,128]{1,0:T(8,128)}, f32[512,128]{1,0:T(8,128)S(1)}) custom-call(f32[1280,128]{1,0:T(8,128)S(1)} %get-tuple-element.9.g_ref, f32[512,128]{1,0:T(8,128)S(1)} %copy-done), custom_call_target="tpu_custom_call" | custom-call | tf_op jit(solution)/shard_map/find_basis/pallas_call | solution.py:401
  64.7 6.8 %find_core.1 = f32[256,32,128]{2,1,0:T(8,128)} custom-call(f32[256,32,512]{2,1,0:T(8,128)S(1)} %get-tuple-element.7.x_ref, f32[128,128]{1,0:T(8,128)S(1)} %get-tuple-element.8.mean_ref, f32[512,128]{1,0:T(8,128)S(1)} %get-tuple-element.10.factor_ref), custom_call_target="tpu_custom_call" | custom-call | tf_op jit(solution)/shard_map/find_core/pallas_call | solution.py:438
Async XLA Ops:
  0.6 39.9 %copy-start = (f32[512,128]{1,0:T(8,128)S(1)}, f32[512,128]{1,0:T(8,128)}, u32[]{:S(2)}) copy-start(f32[512,128]{1,0:T(8,128)} %start_ref.1) | copy-start | bytes 786436

commit v6 on v5

--- a/solution.py
+++ b/solution.py
@@ -305,13 +305,20 @@
         entry = {(i, k): spread(columns[0][k][i : i + 1, :]) for k in range(8) for i in range(k, 8)}
         base = jnp.where(inside, jnp.where(lane == first + sub, 1.0, 0.0), tiles[panel])
         scale, rows = [], []
-        for k in range(8):
-            scale.append(lax.rsqrt(entry[k, k]))
+        for k in range(0, 8, 2):
+            pivot, beside = entry[k, k], entry[k + 1, k]
+            det = pivot * entry[k + 1, k + 1] - beside * beside
+            first_scale = lax.rsqrt(pivot)
+            scale += [first_scale, (pivot * first_scale) * lax.rsqrt(det)]
             for i in range(k + 1, 8):
-                entry[i, k] = entry[i, k] * scale[k]
-            for j in range(k + 1, 8):
+                entry[i, k] = entry[i, k] * first_scale
+            for i in range(k + 2, 8):
+                entry[i, k + 1] = (entry[i, k + 1] - entry[i, k] * entry[k + 1, k]) * scale[k + 1]
+            for j in range(k + 2, 8):
                 for i in range(j, 8):
-                    entry[i, j] = entry[i, j] - entry[i, k] * entry[j, k]
+                    entry[i, j] = (entry[i, j] - entry[i, k] * entry[j, k]) - (
+                        entry[i, k + 1] * entry[j, k + 1]
+                    )
         for k in range(8):
             row = spread(base[k : k + 1, :])
             for i in range(k):
@@ -355,24 +362,34 @@
     return jnp.dot(a, b, preferred_element_type=F32)
 
 
-def basis_kernel(scale, g_ref, start_ref, out_ref, kept, gram1, gram2, gram3):
+def basis_kernel(g_ref, start_ref, out_ref, kept, gram):
     loci, rank = start_ref.shape
+    on = lax.broadcasted_iota(jnp.int32, (LANES, LANES), 0) == lax.broadcasted_iota(
+        jnp.int32, (LANES, LANES), 1
+    )
+    largest = jnp.zeros((LANES, LANES), F32)
+    for index, (i, j) in enumerate(pairs(loci)):
+        if i == j:
+            block = g_ref[index * LANES : (index + 1) * LANES, :]
+            largest = jnp.maximum(largest, jnp.where(on, block, 0.0))
+    largest = jnp.max(jnp.max(largest, axis=0, keepdims=True), axis=1, keepdims=True)
+    scale = 1.0 / largest
     for index, (i, j) in enumerate(pairs(loci)):
         block = g_ref[index * LANES : (index + 1) * LANES, :] * scale
         rows, cols = slice(i * LANES, (i + 1) * LANES), slice(j * LANES, (j + 1) * LANES)
-        for ref, piece in zip((gram1, gram2, gram3), split3(block)):
-            ref[rows, cols] = piece
+        for at, piece in zip((loci, 2 * loci, 0), split3(block)):
+            gram[rows, at + j * LANES : at + (j + 1) * LANES] = piece
         if i != j:
-            for ref, piece in zip((gram1, gram2, gram3), split3(block.T)):
-                ref[cols, rows] = piece
+            for at, piece in zip((loci, 2 * loci, 0), split3(block.T)):
+                gram[cols, at + i * LANES : at + (i + 1) * LANES] = piece
     out_ref[...] = start_ref[...]
 
     def step(_, carry):
         q1, q2, q3 = split3(out_ref[...])
         both = jnp.concatenate([q1, q2], axis=1)
-        large, small = dot16(gram1[...], both), dot16(gram2[...], both)
-        rest = dot16(gram1[...], q3) + dot16(gram3[...], q1)
-        z = large[:, :rank] + (large[:, rank:] + (small[:, :rank] + (small[:, rank:] + rest)))
+        large = dot16(gram[:, loci:], jnp.concatenate([both, both], axis=0))
+        rest = dot16(gram[:, : 2 * loci], jnp.concatenate([q1, q3], axis=0))
+        z = large[:, :rank] + (large[:, rank:] + rest)
         z1, z2, z3 = split3(z)
         both = jnp.concatenate([z1, z2], axis=1)
         square = tdot16(both, both)
@@ -380,33 +397,34 @@
         rest = rest + rest.T + square[rank:, rank:]
         small = square[:rank, :rank] + (square[:rank, rank:] + (square[rank:, :rank] + rest))
         w1, w2, w3 = split3(inverse_lower(small))
+        none = jnp.zeros_like(w1)
         right = jnp.concatenate(
-            [jnp.concatenate([w1, w1], axis=1), jnp.concatenate([w2, w2], axis=1)], axis=0
+            [
+                jnp.concatenate([w1, w1, w1, w3], axis=1),
+                jnp.concatenate([w2, w2, none, none], axis=1),
+            ],
+            axis=0,
         )
-        contract = (((1,), (1,)), ((), ()))
-        large = lax.dot_general(both, right, contract, preferred_element_type=F32)
-        rest = lax.dot_general(
-            jnp.concatenate([z3, z1], axis=1), jnp.concatenate([w1, w3], axis=1), contract,
+        large = lax.dot_general(
+            jnp.concatenate([z1, z2, z3, z1], axis=1), right, (((1,), (1,)), ((), ())),
             preferred_element_type=F32,
         )
-        out_ref[...] = large[:, :rank] + (large[:, rank:] + rest)
+        out_ref[...] = large[:, :rank] + large[:, rank:]
         return carry
 
     lax.fori_loop(0, ITERS, step, 0)
     kept[...] = out_ref[...]
 
 
-def find_basis(gram, start, scale):
+def find_basis(gram, start):
     loci, rank = start.shape
     return pl.pallas_call(
-        functools.partial(basis_kernel, scale),
+        basis_kernel,
         in_specs=[pl.BlockSpec(memory_space=pltpu.VMEM)] * 2,
         out_specs=[pl.BlockSpec(memory_space=pltpu.VMEM)] * 2,
         out_shape=[jax.ShapeDtypeStruct(start.shape, F32), pltpu.VMEM(start.shape, F32)],
         scratch_shapes=[
-            pltpu.VMEM((loci, loci), BF16),
-            pltpu.VMEM((loci, loci), BF16),
-            pltpu.VMEM((loci, loci), BF16),
+            pltpu.VMEM((loci, 3 * loci), BF16),
         ],
         compiler_params=pltpu.CompilerParams(vmem_limit_bytes=30 * 2**20),
         name="find_basis",
@@ -421,12 +439,13 @@
     )
     fhi, flo = split(factor_ref[...])
     pieces = jnp.concatenate([fhi, flo], axis=1)
+    pieces = jnp.concatenate([pieces, pieces], axis=0)
     part = demes
     first = pl.program_id(0) * demes
     for at in range(0, demes, part):
         hi, lo = split((x_ref[pl.ds(first + at, part)] - mean[None]).reshape(part * gens, loci))
-        both = dot16(hi, pieces)
-        value = both[:, :rank] + (both[:, rank:] + dot16(lo, fhi))
+        both = dot16(jnp.concatenate([hi, lo], axis=1), pieces)
+        value = both[:, :rank] + both[:, rank:]
         out_ref[at : at + part] = value.reshape(part, gens, rank)
 
 
@@ -455,8 +474,7 @@
         unit = 8 * nd * ng
         packed = -(-len(pairs(loci)) * LANES // unit) * unit
         gram, mean, kept = sum_gram(freqs, packed, nd, nx)
-        scale = 1.0 / (demes * nd * gens * ng)
-        factor, near = find_basis(gram, start_basis, scale)
+        factor, near = find_basis(gram, start_basis)
         return find_core(kept, mean, near), factor
 
     in_specs = (P("deme", "gen", None), P())

time: 71.7 us -> 70 us (0.976)
  Pallas kernels: 70.9 us -> 69.2 us
    pallas_call x1, Pallas kernels: 24.2 us -> 22.5 us  [find_basis(): pl.pallas_call(basis_kernel, in_specs=[pl.BlockSpec(memory_space=pltpu.VM...]
where the time goes in v6:
time: 70 us; the launch traced here: 69.8 us
  Pallas kernels  69.2 us (99%)
    pallas_call x1, Pallas kernels, sum_gram(): pl.pallas_call(functools.partial(gram_kernel, nd, nx), in_specs=[pl.Block...  39.8 us
    pallas_call x1, Pallas kernels, find_basis(): pl.pallas_call(basis_kernel, in_specs=[pl.BlockSpec(memory_space=pltpu.VM...  22.5 us
    pallas_call x1, Pallas kernels, find_core(): pl.pallas_call(core_kernel, grid=(demes // tile,), in_specs=[vmem, vmem,...  6.84 us

profile of v6, /device:TPU:0, one launch (start us, length us, event | category | flops | bytes accessed | tf_op | source)
XLA Modules:
  0.0 69.8 jit_solution(18382553552657062367)
XLA Ops:
  0.6 0.0 copy-start
  0.6 39.8 %sum_gram.1 = (f32[1280,128]{1,0:T(8,128)S(1)}, f32[128,128]{1,0:T(8,128)S(1)}, f32[256,32,512]{2,1,0:T(8,128)S(1)}) custom-call(f32[256,32,512]{2,1,0:T(8,128)} %x_ref.1), custom_call_target="tpu_custom_call" | custom-call | tf_op jit(solution)/shard_map/sum_gram/pallas_call | solution.py:255
  40.5 0.0 copy-done
  40.5 22.5 %find_basis.1 = (f32[512,128]{1,0:T(8,128)}, f32[512,128]{1,0:T(8,128)S(1)}) custom-call(f32[1280,128]{1,0:T(8,128)S(1)} %get-tuple-element.9.g_ref, f32[512,128]{1,0:T(8,128)S(1)} %copy-done), custom_call_target="tpu_custom_call" | custom-call | tf_op jit(solution)/shard_map/find_basis/pallas_call | solution.py:421
  63.0 6.8 %find_core.1 = f32[256,32,128]{2,1,0:T(8,128)} custom-call(f32[256,32,512]{2,1,0:T(8,128)S(1)} %get-tuple-element.7.x_ref, f32[128,128]{1,0:T(8,128)S(1)} %get-tuple-element.8.mean_ref, f32[512,128]{1,0:T(8,128)S(1)} %get-tuple-element.10.factor_ref), custom_call_target="tpu_custom_call" | custom-call | tf_op jit(solution)/shard_map/find_core/pallas_call | solution.py:457
Async XLA Ops:
  0.6 39.9 %copy-start = (f32[512,128]{1,0:T(8,128)S(1)}, f32[512,128]{1,0:T(8,128)}, u32[]{:S(2)}) copy-start(f32[512,128]{1,0:T(8,128)} %start_ref.1) | copy-start | bytes 786436
